TPU v7x, 256 devices: a whole 4x4x8 slice. The times are simulated.
256 devices in a mesh: shard: 32 (over x_lo, z, core), rep: 8 (over y, x_hi).
Axes of the slice: x: 4 (x_hi: 2, x_lo: 2; x = x_hi * 2 + x_lo), y: 4, z: 8, core: 2. Of those that a mesh axis runs over, the one named last changes fastest.
Arguments:
- tokens: bfloat16 [2, 256, 128, 768], P(None, ('shard', 'rep')), may hold values from -6 to 6
- cotangent: bfloat16 [2, 256, 128, 768], P(None, ('shard', 'rep')), may hold values from -6 to 6
- picture_lengths: int32 [2, 256, 4], P(None, ('shard', 'rep')), may hold values from 1 to 64, 128 in all within a row
- w_qkv: float32 [2, 768, 2304], P(None, 'shard'), may hold values from -0.21875 to 0.21875
- mom_qkv: float32 [2, 768, 2304], P(None, 'shard'), may hold values from -6 to 6
- ema_qkv: float32 [2, 768, 2304], P(None, 'shard'), may hold values from -0.0009765625 to 0.0009765625
- w_out: float32 [2, 768, 768], P(None, 'shard'), may hold values from -0.875 to 0.875
- mom_out: float32 [2, 768, 768], P(None, 'shard'), may hold values from -4 to 4
- ema_out: float32 [2, 768, 768], P(None, 'shard'), may hold values from -0.00390625 to 0.00390625
- w_up: float32 [2, 768, 3072], P(None, 'shard'), may hold values from -0.21875 to 0.21875
- mom_up: float32 [2, 768, 3072], P(None, 'shard'), may hold values from -4 to 4
- ema_up: float32 [2, 768, 3072], P(None, 'shard'), may hold values from -0.0009765625 to 0.0009765625
- w_down: float32 [2, 3072, 768], P(None, 'shard'), may hold values from -0.109375 to 0.109375
- mom_down: float32 [2, 3072, 768], P(None, 'shard'), may hold values from -6 to 6
- ema_down: float32 [2, 3072, 768], P(None, 'shard'), may hold values from -0.00048828125 to 0.00048828125
- norms: float32 [2, 3200], P(None, 'shard'), may hold values from -0.5 to 1.6
- mom_norms: float32 [2, 3200], P(None, 'shard'), may hold values from -6 to 6
- ema_norms: float32 [2, 3200], P(None, 'shard'), may hold values from -0.0025 to 0.008
Outputs:
- activations: bfloat16 [2, 256, 128, 768], P(None, ('shard', 'rep'))
- input_grad: bfloat16 [2, 256, 128, 768], P(None, ('shard', 'rep'))
- new_qkv: float32 [2, 768, 2304], P(None, 'shard')
- new_mom_qkv: float32 [2, 768, 2304], P(None, 'shard')
- new_ema_qkv: float32 [2, 768, 2304], P(None, 'shard')
- copy_qkv: bfloat16 [2, 768, 2304], P(None, 'shard')
- new_out: float32 [2, 768, 768], P(None, 'shard')
- new_mom_out: float32 [2, 768, 768], P(None, 'shard')
- new_ema_out: float32 [2, 768, 768], P(None, 'shard')
- copy_out: bfloat16 [2, 768, 768], P(None, 'shard')
- new_up: float32 [2, 768, 3072], P(None, 'shard')
- new_mom_up: float32 [2, 768, 3072], P(None, 'shard')
- new_ema_up: float32 [2, 768, 3072], P(None, 'shard')
- copy_up: bfloat16 [2, 768, 3072], P(None, 'shard')
- new_down: float32 [2, 3072, 768], P(None, 'shard')
- new_mom_down: float32 [2, 3072, 768], P(None, 'shard')
- new_ema_down: float32 [2, 3072, 768], P(None, 'shard')
- copy_down: bfloat16 [2, 3072, 768], P(None, 'shard')
- new_norms: float32 [2, 3200], P(None, 'shard')
- new_mom_norms: float32 [2, 3200], P(None, 'shard')
- new_ema_norms: float32 [2, 3200], P(None, 'shard')
- copy_norms: bfloat16 [2, 3200], P(None, 'shard')
- shift_gradient: float32 [2, 768], P(None, 'shard')
Inputs may be any that keep to these rules, and one draw needn't show every extreme that they name: `picture_lengths`: each row's lengths sum to 128.
All inputs are finite; a program needn't handle non-finite values.
Results may differ from a plain program's by a relative error of at most 0.03.
Values may be sent and summed in bfloat16 or wider, within the bound.
A program may use at most 256 MiB of HBM per device.

v0:
```python
import jax
import jax.numpy as jnp
from jax import lax
from jax.sharding import PartitionSpec as P

D = 768
HEADS = 12
HD = 64


eps = 1e-06
momentum_decay = 0.9
average_decay = 0.99
learn_rate = 0.03


def in_one_piece(arrays, axis, dim, along):
    ends, at = ([], 0)
    for a in arrays[:-1]:
        at += a.shape[along]
        ends.append(at)
    both = jnp.concatenate(arrays, axis=along)
    return tuple(jnp.split(lax.all_gather(both, axis, axis=dim, tiled=True), ends, axis=along))


def side_by_side(arrays, axis, dim, along):
    widths = [a.shape[along] for a in arrays]
    both = jnp.concatenate(arrays, axis=along)
    filled = lax.psum_scatter(both, axis, scatter_dimension=dim, tiled=True)
    return tuple(jnp.split(filled, [sum(widths[:k]) for k in range(1, len(widths))], axis=along))


def as_sent(x):

    def short(part):
        return part.astype(jnp.bfloat16) if part.dtype == jnp.float32 else part

    return jax.tree.map(short, x)


def layer_norm(values, scale_gain, shift_bias):
    center = values - jnp.mean(values, -1, keepdims=True)
    spread = jnp.mean(center * center, -1, keepdims=True)
    return center * lax.rsqrt(spread + eps) * scale_gain + shift_bias


def head_norm(values, scale_gain):
    center = values - jnp.mean(values, -1, keepdims=True)
    spread = jnp.mean(center * center, -1, keepdims=True)
    return center * lax.rsqrt(spread + eps) * scale_gain


def segment_ids(lengths, length_row):
    picture_ends = jnp.cumsum(lengths)
    places = jnp.arange(length_row, dtype=jnp.int32)
    return jnp.sum((places[:, None] >= picture_ends[None, :]).astype(jnp.int32), 1)


def split_params(norm_params):
    return (
        norm_params[0:D],
        norm_params[D : 2 * D],
        norm_params[2 * D : 3 * D],
        norm_params[3 * D : 4 * D],
        norm_params[4 * D : 4 * D + HD],
        norm_params[4 * D + HD :],
    )


def attention_scores(queries, keys_low, same_picture):
    scores = jnp.einsum(
        "qhd,khd->hqk", queries, keys_low, preferred_element_type=jnp.float32
    ) * HD ** (-0.5)
    return jnp.where(same_picture[None], scores, -1e30)


def forward_layer(stream, same_picture, weights):
    w_qkv, w_out, w_up, w_down, norm_params = weights
    gain_one, shift_one, gain_two, shift_two, gain_query, gain_key = split_params(
        norm_params.astype(jnp.float32)
    )
    length_row = stream.shape[0]
    normed = layer_norm(stream, gain_one, shift_one).astype(jnp.bfloat16)
    joined = jnp.dot(normed, w_qkv, preferred_element_type=jnp.float32).reshape(
        length_row, 3, HEADS, HD
    )
    raw_query = joined[:, 0]
    raw_key = joined[:, 1]
    queries = head_norm(raw_query, gain_query).astype(jnp.bfloat16)
    keys_low = head_norm(raw_key, gain_key).astype(jnp.bfloat16)
    values_low = joined[:, 2].astype(jnp.bfloat16)
    scores = attention_scores(queries, keys_low, same_picture)
    row_top = jnp.max(scores, -1, keepdims=True)
    exponent = jnp.exp(scores - row_top)
    row_total = jnp.sum(exponent, -1, keepdims=True)
    probability = (exponent / row_total).astype(jnp.bfloat16)
    log_total = row_top + jnp.log(row_total)
    mixed = jnp.einsum("hqk,khd->qhd", probability, values_low, preferred_element_type=jnp.float32)
    mixed = mixed.reshape(length_row, D).astype(jnp.bfloat16)
    middle = stream + jnp.dot(mixed, w_out, preferred_element_type=jnp.float32)
    second = layer_norm(middle, gain_two, shift_two).astype(jnp.bfloat16)
    before = jnp.dot(second, w_up, preferred_element_type=jnp.float32)
    hidden = jax.nn.gelu(before).astype(jnp.bfloat16)
    output = middle + jnp.dot(hidden, w_down, preferred_element_type=jnp.float32)
    kept_values = (
        stream,
        normed,
        raw_query,
        raw_key,
        queries,
        keys_low,
        values_low,
        log_total,
        mixed,
        middle,
        second,
        before,
        hidden,
    )
    return (output, kept_values)


def backward_layer(gradient, kept_values, same_picture, weights):
    w_qkv, w_out, w_up, w_down, norm_params = weights
    gain_one, shift_one, gain_two, shift_two, gain_query, gain_key = split_params(
        norm_params.astype(jnp.float32)
    )
    (
        stream,
        normed,
        raw_query,
        raw_key,
        queries,
        keys_low,
        values_low,
        log_total,
        mixed,
        middle,
        second,
        before,
        hidden,
    ) = kept_values
    length_row = stream.shape[0]
    grad_low = gradient.astype(jnp.bfloat16)
    grad_down = jnp.dot(hidden.T, grad_low, preferred_element_type=jnp.float32)
    grad_hidden = jnp.dot(grad_low, w_down.T, preferred_element_type=jnp.float32)
    unused, gelu_pull = jax.vjp(jax.nn.gelu, before)
    grad_before = gelu_pull(grad_hidden)[0].astype(jnp.bfloat16)
    grad_up = jnp.dot(second.T, grad_before, preferred_element_type=jnp.float32)
    grad_second = jnp.dot(grad_before, w_up.T, preferred_element_type=jnp.float32)
    unused, second_pull = jax.vjp(layer_norm, middle, gain_two, shift_two)
    grad_middle, grad_gain_two, grad_shift_two = second_pull(grad_second)
    grad_middle = gradient + grad_middle
    middle_low = grad_middle.astype(jnp.bfloat16)
    grad_out = jnp.dot(mixed.T, middle_low, preferred_element_type=jnp.float32)
    grad_mixed = jnp.dot(middle_low, w_out.T, preferred_element_type=jnp.float32)
    grad_mixed = grad_mixed.reshape(length_row, HEADS, HD).astype(jnp.bfloat16)
    scores = attention_scores(queries, keys_low, same_picture)
    probability = jnp.where(same_picture[None], jnp.exp(scores - log_total), 0.0)
    grad_values = jnp.einsum(
        "hqk,qhd->khd",
        probability.astype(jnp.bfloat16),
        grad_mixed,
        preferred_element_type=jnp.float32,
    )
    grad_probs = jnp.einsum(
        "qhd,khd->hqk", grad_mixed, values_low, preferred_element_type=jnp.float32
    )
    inner_sum = jnp.sum(grad_probs * probability, -1, keepdims=True)
    grad_scores = (probability * (grad_probs - inner_sum)).astype(jnp.bfloat16)
    grad_query = jnp.einsum(
        "hqk,khd->qhd", grad_scores, keys_low, preferred_element_type=jnp.float32
    ) * HD ** (-0.5)
    grad_key = jnp.einsum(
        "hqk,qhd->khd", grad_scores, queries, preferred_element_type=jnp.float32
    ) * HD ** (-0.5)
    unused, query_pull = jax.vjp(head_norm, raw_query, gain_query)
    grad_raw_query, grad_gain_query = query_pull(grad_query)
    unused, key_pull = jax.vjp(head_norm, raw_key, gain_key)
    grad_raw_key, grad_gain_key = key_pull(grad_key)
    grad_joined = (
        jnp.stack([grad_raw_query, grad_raw_key, grad_values], 1)
        .reshape(length_row, 3 * D)
        .astype(jnp.bfloat16)
    )
    grad_qkv = jnp.dot(normed.T, grad_joined, preferred_element_type=jnp.float32)
    grad_normed = jnp.dot(grad_joined, w_qkv.T, preferred_element_type=jnp.float32)
    unused, first_pull = jax.vjp(layer_norm, stream, gain_one, shift_one)
    grad_stream, grad_gain_one, grad_shift_one = first_pull(grad_normed)
    grad_params = jnp.concatenate(
        [
            grad_gain_one,
            grad_shift_one,
            grad_gain_two,
            grad_shift_two,
            grad_gain_query,
            grad_gain_key,
        ]
    )
    return (grad_middle + grad_stream, (grad_qkv, grad_out, grad_up, grad_down, grad_params))


def body(
    tokens,
    cotangent,
    picture_lengths,
    w_qkv,
    mom_qkv,
    ema_qkv,
    w_out,
    mom_out,
    ema_out,
    w_up,
    mom_up,
    ema_up,
    w_down,
    mom_down,
    ema_down,
    norms,
    mom_norms,
    ema_norms,
):
    masters = (w_qkv, w_out, w_up, w_down, norms)
    lowered = tuple((master.astype(jnp.bfloat16) for master in masters))
    layer_count = w_qkv.shape[0]
    micro_count = tokens.shape[0]
    length_row = tokens.shape[2]
    resident = (
        *in_one_piece((lowered[0], lowered[1], lowered[2]), "shard", 1, 2),
        lax.all_gather(lowered[3], "shard", axis=1, tiled=True),
        lax.all_gather(lowered[4], "shard", axis=1, tiled=True),
    )

    def forward_weights(layer_index):
        return tuple((whole_array[layer_index] for whole_array in resident))

    def backward_weights(layer_index):
        return tuple((whole_array[layer_index] for whole_array in resident))

    summed = tuple(
        (
            jnp.zeros(
                (layer_count, master.shape[1] * lax.axis_size("shard")) + master.shape[2:],
                jnp.float32,
            )
            for master in masters
        )
    ) + (jnp.zeros((layer_count, D), jnp.float32),)
    outputs = []
    grads_in = []
    for micro_index in range(micro_count):
        segments = segment_ids(picture_lengths[micro_index, 0], length_row)
        same_picture = segments[:, None] == segments[None, :]
        stream = tokens[micro_index, 0].astype(jnp.float32)
        kept_all = []
        for layer_index in range(layer_count):
            stream, kept_values = forward_layer(stream, same_picture, forward_weights(layer_index))
            kept_all.append(kept_values)
        outputs.append(stream.astype(jnp.bfloat16))
        gradient = cotangent[micro_index, 0].astype(jnp.float32)
        layer_grads = [None] * layer_count
        for layer_index in reversed(range(layer_count)):
            gradient, layer_grads[layer_index] = backward_layer(
                gradient, kept_all[layer_index], same_picture, backward_weights(layer_index)
            )
        grads_in.append(gradient.astype(jnp.bfloat16))
        stacked = tuple(
            (jnp.stack([entry[kind_index] for entry in layer_grads]) for kind_index in range(5))
        )
        stacked = stacked + (stacked[4][:, 3 * D : 4 * D],)
        summed = tuple((running + fresh for running, fresh in zip(summed, stacked)))
    shares = (
        *tuple(
            (
                part.astype(jnp.float32)
                for part in side_by_side(
                    (
                        summed[0].astype(jnp.bfloat16),
                        summed[1].astype(jnp.bfloat16),
                        summed[2].astype(jnp.bfloat16),
                    ),
                    "shard",
                    1,
                    2,
                )
            )
        ),
        lax.psum_scatter(
            summed[3].astype(jnp.bfloat16), "shard", scatter_dimension=1, tiled=True
        ).astype(jnp.float32),
        lax.psum_scatter(
            summed[4].astype(jnp.bfloat16), "shard", scatter_dimension=1, tiled=True
        ).astype(jnp.float32),
        lax.psum_scatter(
            summed[5].astype(jnp.bfloat16), "shard", scatter_dimension=1, tiled=True
        ).astype(jnp.float32),
    )
    totals = jax.tree.map(lambda part: part.astype(jnp.float32), lax.psum(as_sent(shares), "rep"))
    token_count = (
        micro_count * tokens.shape[1] * length_row * lax.axis_size("shard") * lax.axis_size("rep")
    )
    factor = token_count ** (-0.5)
    moments = (mom_qkv, mom_out, mom_up, mom_down, mom_norms)
    averages = (ema_qkv, ema_out, ema_up, ema_down, ema_norms)
    results = [jnp.stack(outputs)[:, None], jnp.stack(grads_in)[:, None]]
    for master, moment, average, gradient_sum in zip(masters, moments, averages, totals[:5]):
        gradient_scaled = gradient_sum * factor
        moment_new = momentum_decay * moment + gradient_scaled
        master_new = master - learn_rate * (gradient_scaled + momentum_decay * moment_new)
        average_new = average_decay * average + (1.0 - average_decay) * master_new
        results.extend([master_new, moment_new, average_new, master_new.astype(jnp.bfloat16)])
    results.append(totals[5] * factor)
    return tuple(results)


def solution(mesh):
    return jax.shard_map(
        body,
        mesh=mesh,
        in_specs=(
            P(None, ("shard", "rep"), None, None),
            P(None, ("shard", "rep"), None, None),
            P(None, ("shard", "rep"), None),
            P(None, "shard", None),
            P(None, "shard", None),
            P(None, "shard", None),
            P(None, "shard", None),
            P(None, "shard", None),
            P(None, "shard", None),
            P(None, "shard", None),
            P(None, "shard", None),
            P(None, "shard", None),
            P(None, "shard", None),
            P(None, "shard", None),
            P(None, "shard", None),
            P(None, "shard"),
            P(None, "shard"),
            P(None, "shard"),
        ),
        out_specs=(
            P(None, ("shard", "rep"), None, None),
            P(None, ("shard", "rep"), None, None),
            P(None, "shard", None),
            P(None, "shard", None),
            P(None, "shard", None),
            P(None, "shard", None),
            P(None, "shard", None),
            P(None, "shard", None),
            P(None, "shard", None),
            P(None, "shard", None),
            P(None, "shard", None),
            P(None, "shard", None),
            P(None, "shard", None),
            P(None, "shard", None),
            P(None, "shard", None),
            P(None, "shard", None),
            P(None, "shard", None),
            P(None, "shard", None),
            P(None, "shard"),
            P(None, "shard"),
            P(None, "shard"),
            P(None, "shard"),
            P(None, "shard"),
        ),
        check_vma=False,
    )
```

profile of v0, /device:TPU:1, one launch (start us, length us, event | category | flops | bytes accessed | tf_op | source)
XLA Modules:
  0.0 840.2 jit_solution(8792636297650856607)
XLA Ops:
  12.2 38.3 %all-gather = bf16[32,100,2]{1,2,0:T(2,128)(2,1)S(1)} all-gather(bf16[1,100,2]{1,2,0:T(2,128)(2,1)S(1)} %convert_bitcast_fusion.2), channel_id=1, replica_groups=mesh['shard'=32,'rep'=8] {'shard'}, dimensions={0}, use_global_device_ids=true | all-gather | bytes 13200 | tf_op jit(solution)/shard_map/all_gather | solution.py:231
  56.5 69.5 %all-gather.4.cloned.1.call-done = bf16[2,768,6144]{2,1,0:T(8,128)(2,1)} async-done(((bf16[2,24,6144]{2,1,0:T(8,128)(2,1)}), bf16[2,768,6144]{2,1,0:T(8,128)(2,1)}) %all-gather.4.cloned.1.call-update) | async-done | bytes 18874384 | tf_op jit(solution)/shard_map/all_gather | solution.py:23
  126.0 5.4 slice_bitcast_fusion.20
  131.4 3.6 copy.107
  135.0 4.7 copy.109
  139.7 3.5 fusion.158
  145.9 1.8 fusion.263
  149.1 4.5 fusion.14
  153.5 48.8 %all-gather.6.cloned.1.call-done = bf16[2,3072,768]{2,1,0:T(8,128)(2,1)} async-done(((bf16[2,96,768]{2,1,0:T(8,128)(2,1)}), bf16[2,3072,768]{2,1,0:T(8,128)(2,1)}) %all-gather.6.cloned.1.call-update) | async-done | bytes 9437200 | tf_op jit(solution)/shard_map/all_gather | solution.py:230
  202.3 4.0 fusion.264
  214.3 2.2 fusion.268
  216.7 3.2 fusion.15
  220.0 4.1 fusion.269
  230.4 4.8 fusion.59
  235.2 1.7 fusion.20
  236.9 4.2 fusion.45
  241.1 2.4 multiply_reduce_fusion.7
  253.8 2.0 multiply_reduce_fusion.8
  257.8 4.2 fusion.52
  263.8 4.2 fusion.38
  268.1 2.4 multiply_reduce_fusion.9
  275.8 5.2 convolution_bitcast_fusion.6
  281.0 5.1 convolution_bitcast_fusion.7
  286.2 5.1 convolution_bitcast_fusion.4
  291.3 5.0 convolution_bitcast_fusion.5
  298.8 4.1 convolution_bitcast_fusion.10
  302.9 4.1 convolution_bitcast_fusion.8
  310.9 2.1 fusion.3
  313.1 4.4 copy.125
  319.2 4.8 convolution_bitcast_fusion.11
  325.6 4.2 convolution_bitcast_fusion.9
  329.8 10.6 %fusion = bf16[2,768,3072]{2,1,0:T(8,128)(2,1)S(1)} fusion(f32[1,768,3072]{2,1,0:T(8,128)S(1)} %bitcast.711, f32[1,768,3072]{2,1,0:T(8,128)} %convolution_bitcast_fusion.7, f32[1,768,3072]{2,1,0:T(8,128)} %convolution_bitcast_fusion.4, f32[1,768,3072]{2,1,0:T(8,128)} %convolution_bitcast_fusion.5), kind=kLoop, calls=%fused_computation.1 | loop fusion | flops 18874368 | bytes 47185920 | tf_op jit(solution)/shard_map/convert_element_type | solution.py:280
  340.4 10.4 %fusion.2 = bf16[2,768,2304]{2,1,0:T(8,128)(2,1)} fusion(f32[1,768,2304]{2,1,0:T(8,128)S(1)} %bitcast.717, f32[1,768,2304]{2,1,0:T(8,128)} %convolution_bitcast_fusion.11, f32[1,768,2304]{2,1,0:T(8,128)} %convolution_bitcast_fusion.8, f32[1,768,2304]{2,1,0:T(8,128)} %convolution_bitcast_fusion.9), kind=kLoop, calls=%fused_computation.6 | loop fusion | flops 14155776 | bytes 35389440 | tf_op jit(solution)/shard_map/convert_element_type | solution.py:278
  350.8 8.8 %pad_maximum_fusion = bf16[2,768,6144]{2,1,0:T(8,128)(2,1)S(1)} fusion(bf16[2,768,3072]{2,1,0:T(8,128)(2,1)S(1)} %fusion, bf16[2,768,768]{2,1,0:T(8,128)(2,1)S(1)} %copy-done.11, bf16[2,768,2304]{2,1,0:T(8,128)(2,1)} %fusion.2), kind=kLoop, calls=%fused_computation.2 | loop fusion | flops 56623104 | bytes 37748736 | tf_op jit(solution)/shard_map/concatenate | solution.py:28
  359.6 77.2 %copy.148 = bf16[2,768,6144]{2,0,1:T(2,128)(2,1)} copy(bf16[2,768,6144]{2,1,0:T(8,128)(2,1)S(1)} %pad_maximum_fusion) | data formatting | bytes 37748736
  436.8 20.4 %copy.157 = bf16[96,8,2,6144]{3,1,2,0:T(8,128)(2,1)} copy(bf16[96,8,2,6144]{3,2,1,0:T(2,128)(2,1)} %bitcast.709) | data formatting | bytes 37748736
  458.2 3.1 convolution_bitcast_fusion.2
  464.5 5.1 convolution_bitcast_fusion.1
  469.7 9.8 %fusion.1 = bf16[2,3072,768]{2,1,0:T(8,128)(2,1)} fusion(f32[1,3072,768]{2,1,0:T(8,128)S(1)} %convolution_bitcast_fusion.2, f32[1,3072,768]{2,1,0:T(8,128)S(1)} %convolution_bitcast_fusion.3, f32[1,3072,768]{2,1,0:T(8,128)S(1)} %convolution_bitcast_fusion, f32[1,3072,768]{2,1,0:T(8,128)} %convolution_bitcast_fusion.1), kind=kLoop, calls=%fused_computation.4 | loop fusion | flops 18874368 | bytes 47185920 | tf_op jit(solution)/shard_map/convert_element_type | solution.py:289
  482.2 3.4 fusion.10
  485.7 3.5 fusion.101
  490.3 103.1 %all-reduce.2 = (bf16[2,3200]{1,0:T(2,128)(2,1)S(1)}, bf16[2,768]{1,0:T(2,128)(2,1)S(1)}) all-reduce(bf16[2,3200]{1,0:T(2,128)(2,1)S(1)} %fusion.199, bf16[2,768]{1,0:T(2,128)(2,1)S(1)} %fusion.211), channel_id=4, replica_groups=mesh['shard'=32,'rep'=8] {'shard'}, use_global_device_ids=true, to_apply=%region_110.111.clone | all-reduce | flops 7936 | bytes 31744
  593.6 21.3 %all-reduce.3 = (bf16[2,100]{1,0:T(2,128)(2,1)S(1)}, bf16[2,24]{1,0:T(2,128)(2,1)S(1)}) all-reduce(bf16[2,100]{1,0:T(2,128)(2,1)S(1)} %constant_dynamic-slice_fusion.1, bf16[2,24]{1,0:T(2,128)(2,1)S(1)} %constant_dynamic-slice_fusion), channel_id=1, replica_groups=mesh['shard'=32,'rep'=8] {'rep'}, use_global_device_ids=true, to_apply=%region_111.112 | all-reduce | flops 248 | bytes 992 | tf_op jit(solution)/shard_map/psum | solution.py:298
  615.2 4.0 fusion.77
  619.3 3.4 fusion.76
  626.8 103.3 %reduce-scatter.7.cloned.1.call-done = bf16[2,96,768]{2,1,0:T(8,128)(2,1)} async-done(((bf16[2,3072,768]{2,1,0:T(8,128)(2,1)}), bf16[2,96,768]{2,1,0:T(8,128)(2,1)}) %reduce-scatter.7.cloned.1.call-update) | async-done | bytes 294928 | tf_op jit(solution)/shard_map/reduce_scatter | solution.py:288
  733.4 90.6 %all-reduce.7.cloned.1.call-done = (bf16[2,24,2304]{2,1,0:T(8,128)(2,1)}, bf16[2,24,768]{2,1,0:T(8,128)(2,1)}, bf16[2,24,3072]{2,1,0:T(8,128)(2,1)}, bf16[2,96,768]{2,1,0:T(8,128)(2,1)}) async-done(((bf16[2,24,2304]{2,1,0:T(8,128)(2,1)}, bf16[2,24,768]{2,1,0:T(8,128)(2,1)}, bf16[2,24,3072]{2,1,0:T(8,128)(2,1)}, bf16[2,96,768]{2,1,0:T(8,128)(2,1)}), (bf16[2,24,2304]{2,1,0:T(8,128)(2,1)}, ...) | async-done | bytes 884752 | tf_op jit(solution)/shard_map/psum | solution.py:298
  824.0 1.9 fusion.254
  (597 shorter events, 78.1 us)
Async XLA Ops:
  7.2 118.8 %all-gather.4.cloned.1.call-start = ((), (), s32[]{:S(2)}) async-start(), calls=%async_computation.2 | async-start | bytes 19464192 | tf_op jit(solution)/shard_map/all_gather | solution.py:23
  10.4 40.2 %copy-start.158 = (s32[2,1,4]{2,1,0:T(1,128)S(1)}, s32[2,1,4]{2,1,0:T(1,128)}, u32[]{:S(2)}) copy-start(s32[2,1,4]{2,1,0:T(1,128)} %param.20) | copy-start | bytes 100
  10.4 41.4 %copy-start.1 = (bf16[2,1,128,768]{3,2,1,0:T(8,128)(2,1)S(1)}, bf16[2,1,128,768]{3,2,1,0:T(8,128)(2,1)}, u32[]{:S(2)}) copy-start(bf16[2,1,128,768]{3,2,1,0:T(8,128)(2,1)} %param.18) | copy-start | bytes 1179652
  11.3 191.0 %all-gather.6.cloned.1.call-start = ((), (), s32[]{:S(2)}) async-start(), calls=%async_computation.3 | async-start | bytes 9732096 | tf_op jit(solution)/shard_map/all_gather | solution.py:230
  12.1 610.6 %reduce-scatter.9.cloned.1.call-start = ((), (), s32[]{:S(2)}) async-start(), calls=%async_computation.5 | async-start | bytes 19464192
  202.3 4.8 copy-start.66
  202.3 4.8 copy-start.69
  212.7 97.4 %copy-start.7 = (f32[128,3,12,64]{0,3,2,1:T(8,128)}, f32[128,3,12,64]{0,3,2,1:T(8,128)S(1)}, u32[]{:S(2)}) copy-start(f32[128,3,12,64]{0,3,2,1:T(8,128)S(1)} %fusion.162) | copy-start | bytes 3538948
  212.8 96.5 %copy-start.92 = (f32[128,12]{0,1:T(8,128)}, f32[128,12]{0,1:T(8,128)S(1)}, u32[]{:S(2)}) copy-start(f32[128,12]{0,1:T(8,128)S(1)} %broadcast_multiply_fusion.6) | copy-start | bytes 18436
  212.8 97.2 %copy-start.82 = (f32[128,12]{0,1:T(8,128)}, f32[128,12]{0,1:T(8,128)S(1)}, u32[]{:S(2)}) copy-start(f32[128,12]{0,1:T(8,128)S(1)} %broadcast_multiply_fusion.7) | copy-start | bytes 18436
  213.5 96.6 %copy-start.90 = (f32[128,12]{0,1:T(8,128)}, f32[128,12]{0,1:T(8,128)S(1)}, u32[]{:S(2)}) copy-start(f32[128,12]{0,1:T(8,128)S(1)} %fusion.200) | copy-start | bytes 18436
  213.5 13.4 %slice-start.5 = ((s8[18874368]{0:T(1024)(128)(4,1)}), s8[4194304]{0:T(1024)(128)(4,1)S(1)}, s32[]{:S(2)}) async-start(s8[18874368]{0:T(1024)(128)(4,1)} %bitcast.718), calls=%async_computation.12 | async-start | bytes 8388608
  214.3 12.5 %slice-start.6 = ((s8[18874368]{0:T(1024)(128)(4,1)}), s8[4194304]{0:T(1024)(128)(4,1)S(1)}, s32[]{:S(2)}) async-start(s8[18874368]{0:T(1024)(128)(4,1)} %bitcast.718), calls=%async_computation.13 | async-start | bytes 8388608
  220.0 43.8 %copy-start.32 = (f32[128,3072]{1,0:T(8,128)}, f32[128,3072]{1,0:T(8,128)S(1)}, u32[]{:S(2)}) copy-start(f32[128,3072]{1,0:T(8,128)S(1)} %fusion.15) | copy-start | bytes 4718596
  220.0 6.9 slice-start.7
  220.0 6.9 slice-start.8
  228.0 47.8 %copy-start.12 = (f32[128,768]{1,0:T(8,128)}, f32[128,768]{1,0:T(8,128)S(1)}, u32[]{:S(2)}) copy-start(f32[128,768]{1,0:T(8,128)S(1)} %get-tuple-element.296) | copy-start | bytes 1179652
  230.4 6.5 copy-start.26
  256.4 14.5 %copy-start.20 = (f32[128,768]{1,0:T(8,128)}, f32[128,768]{1,0:T(8,128)S(1)}, u32[]{:S(2)}) copy-start(f32[128,768]{1,0:T(8,128)S(1)} %get-tuple-element.243) | copy-start | bytes 1179652
  256.4 17.1 %copy-start.22 = (f32[128,768]{1,0:T(8,128)}, f32[128,768]{1,0:T(8,128)S(1)}, u32[]{:S(2)}) copy-start(f32[128,768]{1,0:T(8,128)S(1)} %get-tuple-element.242) | copy-start | bytes 1179652
  271.0 26.9 %copy-start.16 = (f32[128,768]{1,0:T(8,128)}, f32[128,768]{1,0:T(8,128)S(1)}, u32[]{:S(2)}) copy-start(f32[128,768]{1,0:T(8,128)S(1)} %add_add_fusion.16) | copy-start | bytes 1179652
  273.7 23.1 %copy-start.18 = (f32[128,768]{1,0:T(8,128)}, f32[128,768]{1,0:T(8,128)S(1)}, u32[]{:S(2)}) copy-start(f32[128,768]{1,0:T(8,128)S(1)} %add_add_fusion.19) | copy-start | bytes 1179652
  281.0 5.2 copy-start.53
  313.1 4.4 copy-start.8
  313.1 4.4 copy-start.83
  313.1 4.4 copy-start.91
  313.1 4.4 copy-start.93
  319.0 5.0 copy-start.46
  319.1 5.0 copy-start.48
  319.1 4.9 copy-start.34
  319.2 10.5 %slice-start = ((s8[9437184]{0:T(1024)(128)(4,1)}), s8[4194304]{0:T(1024)(128)(4,1)S(1)}, s32[]{:S(2)}) async-start(s8[9437184]{0:T(1024)(128)(4,1)} %bitcast.710), calls=%async_computation.7 | async-start | bytes 8388608
  319.2 10.5 %slice-start.1 = ((s8[9437184]{0:T(1024)(128)(4,1)}), s8[4194304]{0:T(1024)(128)(4,1)S(1)}, s32[]{:S(2)}) async-start(s8[9437184]{0:T(1024)(128)(4,1)} %bitcast.710), calls=%async_computation.8 | async-start | bytes 8388608
  325.5 14.8 %slice-start.3 = ((s8[7077888]{0:T(1024)(128)(4,1)}), s8[4194304]{0:T(1024)(128)(4,1)S(1)}, s32[]{:S(2)}) async-start(s8[7077888]{0:T(1024)(128)(4,1)} %bitcast.716), calls=%async_computation.10 | async-start | bytes 8388608
  329.8 10.6 %slice-start.4 = ((s8[7077888]{0:T(1024)(128)(4,1)}), s8[2883584]{0:T(1024)(128)(4,1)S(1)}, s32[]{:S(2)}) async-start(s8[7077888]{0:T(1024)(128)(4,1)} %bitcast.716), calls=%async_computation.11 | async-start | bytes 5767168
  340.4 10.4 %copy-start.11 = (bf16[2,768,768]{2,1,0:T(8,128)(2,1)S(1)}, bf16[2,768,768]{2,1,0:T(8,128)(2,1)}, u32[]{:S(2)}) copy-start(bf16[2,768,768]{2,1,0:T(8,128)(2,1)} %copy.125) | copy-start | bytes 7077892
  457.2 272.9 %reduce-scatter.7.cloned.1.call-start = ((), (), s32[]{:S(2)}) async-start(), calls=%async_computation.4 | async-start | bytes 9732096 | tf_op jit(solution)/shard_map/reduce_scatter | solution.py:288
  479.6 344.4 %all-reduce.7.cloned.1.call-start = ((), (), s32[]{:S(2)}) async-start(), calls=%async_computation.6 | async-start | bytes 1769472 | tf_op jit(solution)/shard_map/psum | solution.py:298
  485.7 4.3 copy-start.145
  485.7 4.3 copy-start.146
  489.2 125.6 %copy-start.17 = (f32[128,768]{1,0:T(8,128)S(1)}, f32[128,768]{1,0:T(8,128)}, u32[]{:S(2)}) copy-start(f32[128,768]{1,0:T(8,128)} %copy-done.16) | copy-start | bytes 1179652
  489.3 125.6 %copy-start.19 = (f32[128,768]{1,0:T(8,128)S(1)}, f32[128,768]{1,0:T(8,128)}, u32[]{:S(2)}) copy-start(f32[128,768]{1,0:T(8,128)} %copy-done.18) | copy-start | bytes 1179652
  625.4 106.9 %copy-start.155 = (f32[2,100]{1,0:T(2,128)S(1)}, f32[2,100]{1,0:T(2,128)}, u32[]{:S(2)}) copy-start(f32[2,100]{1,0:T(2,128)} %param.33) | copy-start | bytes 2404
  625.4 106.9 %copy-start.156 = (f32[2,100]{1,0:T(2,128)S(1)}, f32[2,100]{1,0:T(2,128)}, u32[]{:S(2)}) copy-start(f32[2,100]{1,0:T(2,128)} %param.34) | copy-start | bytes 2404
  626.0 106.8 %copy-start.157 = (f32[2,100]{1,0:T(2,128)S(1)}, f32[2,100]{1,0:T(2,128)}, u32[]{:S(2)}) copy-start(f32[2,100]{1,0:T(2,128)} %param.35) | copy-start | bytes 2404
  626.0 197.9 %copy-start.43 = (f32[2,24,2304]{2,1,0:T(8,128)S(1)}, f32[2,24,2304]{2,1,0:T(8,128)}, u32[]{:S(2)}) copy-start(f32[2,24,2304]{2,1,0:T(8,128)} %param.21) | copy-start | bytes 1327108
  626.0 197.9 %copy-start.71 = (f32[2,24,2304]{2,1,0:T(8,128)S(1)}, f32[2,24,2304]{2,1,0:T(8,128)}, u32[]{:S(2)}) copy-start(f32[2,24,2304]{2,1,0:T(8,128)} %param.22) | copy-start | bytes 1327108
  730.9 95.0 %copy-start.70 = (f32[2,24,2304]{2,1,0:T(8,128)S(1)}, f32[2,24,2304]{2,1,0:T(8,128)}, u32[]{:S(2)}) copy-start(f32[2,24,2304]{2,1,0:T(8,128)} %param.23) | copy-start | bytes 1327108
  732.8 94.0 %copy-start.151 = (f32[2,100]{1,0:T(2,128)}, f32[2,100]{1,0:T(2,128)S(1)}, u32[]{:S(2)}) copy-start(f32[2,100]{1,0:T(2,128)S(1)} %get-tuple-element.202) | copy-start | bytes 2404
  (145 other events, 290.3 us)
Sparse Core Ops, SparseCore 0:
  11.4 114.5 all-gather.3
  128.4 73.8 all-gather.5
  457.4 144.4 reduce-scatter.8
  604.3 125.8 reduce-scatter.6
  734.6 89.3 all-reduce.6
where the time goes:
time: 849 us; the launch traced here: 840 us
  waiting for transfers between devices  312 us (37%)
  blocking collectives  163 us (19%)
  matrix products  137 us (16%)
  local copies, waits for them, and re-layouts  136 us (16%)
  other arithmetic  72.7 us (9%)
  between operations  18.7 us (2%)
    unnamed x386, local copies, waits for them, and re-layouts  115 us
    reduce_scatter x1, waiting for transfers between devices, body(): lax.psum_scatter(summed[3].astype(jnp.bfloat16), 'shard', scatter_dimensi...  103 us
    unnamed x1, blocking collectives  103 us
    psum x1, waiting for transfers between devices, body(): lax.psum(as_sent(shares), 'rep')  90.6 us
    all_gather x1, waiting for transfers between devices, in_one_piece(): lax.all_gather(both, axis, axis=dim, tiled=True)  69.5 us
    all_gather x1, waiting for transfers between devices, body(): lax.all_gather(lowered[3], 'shard', axis=1, tiled=True)  48.8 us
    all_gather x1, blocking collectives, body(): lax.all_gather(lowered[4], 'shard', axis=1, tiled=True)  38.3 us
    psum x1, blocking collectives, body(): lax.psum(as_sent(shares), 'rep')  21.3 us
  transfers between devices with their start and end apart: 5, of which 4 were waited for; matrix products, arithmetic and copies ran while one was open for 9% of the time, Pallas kernels for 0%

commit v1 on v0

v1 whole, which is shorter than its diff:
```python
import math
from types import SimpleNamespace

import jax
import jax.numpy as jnp
from jax import lax
from jax.experimental import pallas as pl
from jax.experimental.pallas import tpu as pltpu
from jax.sharding import PartitionSpec as P

D = 768
HEADS = 12
HD = 64
FF = 3072
LAYERS = 2
ROWS = 256
PAIRS = HEADS // 2
CHUNK = 64
FOURTH = 768
RING = 8
BLOCK = 48
DBLOCK = 192
WIDE = 6144
HALF = 1536
QUARTER = 128
C_START, C_WIDTH = 512, 384
A_START, A_WIDTH = 1280, 256
STARTS = {"qkvo": 0, "up": 4 * D}
KINDS = ("qkvo", "up", "down")
PLACES = {off: off + 3 for off in range(-3, 5)} | {-4: 7}
GROUPS = ((3, None), (2, 4), (1, 5), (0, 6), (None, 7))
MESH = pl.DeviceIdType.MESH
BF = jnp.bfloat16
F32 = jnp.float32
NT = (((1,), (1,)), ((), ()))
NN = (((1,), (0,)), ((), ()))
TN = (((0,), (0,)), ((), ()))

eps = 1e-06
momentum_decay = 0.9
average_decay = 0.99
learn_rate = 0.03


class Place:
    def __init__(self):
        shard, rep = lax.axis_index("shard"), lax.axis_index("rep")
        self.c = shard % 2
        self.z = (shard // 2) % 8
        self.xl = shard // 16
        self.xh = rep % 2
        self.y = rep // 2
        self.x = self.xh * 2 + self.xl
        self.ys = [(self.y + d) % 4 for d in range(4)]
        self.xs = [((self.x + d) % 2, (self.x + d) % 4 // 2) for d in range(4)]

    def on_y(self, d):
        return self.ys[d % 4]

    def on_x(self, d):
        return self.xs[d % 4]

    def at(self, x=None, y=None, z=None, c=None):
        x = self.x if x is None else x
        y = self.y if y is None else y
        z = self.z if z is None else z
        c = self.c if c is None else c
        return (((x % 2) * 8 + z) * 2 + c, y * 2 + x // 2)

    def neighbours(self):
        sibling = self.at(c=1 - self.c)
        xs = {d: self.at(x=(self.x + d) % 4) for d in (1, -1, 2)}
        ys = {d: self.at(y=(self.y + d) % 4) for d in (1, -1, 2)}
        zs = {d: self.at(z=(self.z + d) % 8) for d in (1, -1)}
        return sibling, xs, ys, zs


class Net:
    def __init__(self, send, recv, someone, ruler):
        self.send, self.recv, self.someone, self.ruler = send, recv, someone, ruler
        self.count, self.sent = 0, []

    def copy(self, src, dst, device, at):
        return pltpu.make_async_remote_copy(
            src_ref=src,
            dst_ref=dst,
            send_sem=self.send.at[at],
            recv_sem=self.recv.at[at],
            device_id=device,
            device_id_type=MESH,
        )

    def reserve(self):
        self.count += 1
        assert self.count <= self.send.shape[0]
        return self.count - 1

    def put(self, src, dst, device):
        copy = self.copy(src, dst, device, self.reserve())
        copy.start()
        self.sent.append(copy)
        return copy

    def batch(self):
        self.sent.append(Batch(self))
        return self.sent[-1]

    def settle(self, most):
        for copy in self.sent[:most]:
            copy.wait_send()
        del self.sent[:most]

    def finish(self):
        self.settle(len(self.sent))


class Batch:
    def __init__(self, net):
        self.net, self.at, self.size = net, net.reserve(), 0

    def put(self, src, dst, device):
        self.net.copy(src, dst, device, self.at).start()
        self.size += math.prod(src.shape)

    def whole(self):
        tiles, ruler = self.size // 2048, self.net.ruler
        for blocks, depth in ((1, 16), (1, 48), (2, 48), (4, 48), (8, 48)):
            width, rest = divmod(tiles, blocks * (depth // 16))
            if rest == 0 and 128 * width <= ruler.shape[2]:
                view = ruler.at[0:blocks, 0:depth, 0 : 128 * width]
                return self.net.copy(view, view, self.net.someone, self.at)
        raise ValueError(tiles)

    def wait_recv(self):
        self.whole().wait_recv()

    def wait_send(self):
        self.whole().wait_send()


def place_of(zb, z):
    return (zb - z + PLACES[0] + 8) % 8


def greet(devices):
    barrier = pltpu.get_barrier_semaphore()
    for device in devices:
        pl.semaphore_signal(barrier, inc=1, device_id=device, device_id_type=MESH)
    return lambda: pl.semaphore_wait(barrier, len(devices))


def lanes(start, size):
    return pl.ds(pl.multiple_of(start, 128), size)


def rows16(start, size):
    return pl.ds(pl.multiple_of(start, 16), size)


def arrive(copies):
    for copy in copies:
        copy.wait_recv()


def dot(a, b, dims=NN):
    return lax.dot_general(a, b, dims, preferred_element_type=F32)


def by_rows(step, carry=0):
    def one(i, carry):
        return step(pl.ds(pl.multiple_of(i * CHUNK, CHUNK), CHUNK), carry)

    return lax.fori_loop(0, ROWS // CHUNK, one, carry)


def stats(values):
    center = values - jnp.mean(values, -1, keepdims=True)
    return center, lax.rsqrt(jnp.mean(center * center, -1, keepdims=True) + eps)


def fold(values):
    return jnp.sum(values.reshape(-1, 8, values.shape[-1]), 0)


def norm_into(out, source, gain, bias):
    def step(r, carry):
        center, scale = stats(source[r, :].astype(F32))
        out[r, :] = (center * scale * gain + bias).astype(BF)
        return carry

    by_rows(step)


def norm_back(source, slope, gain, grad, low):
    def step(r, carry):
        center, scale = stats(source[r, :].astype(F32))
        unit = center * scale
        up = slope[r, :]
        inner = up * gain
        inner_mean = jnp.mean(inner, -1, keepdims=True)
        along = jnp.mean(inner * unit, -1, keepdims=True)
        new = grad[r, :] + scale * (inner - inner_mean - unit * along)
        grad[r, :] = new
        low[r, :] = new.astype(BF)
        return carry[0] + fold(up * unit), carry[1] + fold(up)

    zero = jnp.zeros((8, D), F32)
    sums = by_rows(step, (zero, zero))
    return tuple(jnp.sum(s, 0, keepdims=True) for s in sums)


def head_mean(values, spread):
    high = values.astype(BF)
    low = (values - high.astype(F32)).astype(BF)
    return dot(jnp.concatenate([high, low], 1), spread)


def split_heads(values, first):
    zero = jnp.zeros_like(values)
    return jnp.concatenate([jnp.where(first, values, zero), jnp.where(first, zero, values)], 0)


def join_heads(values, first):
    half = values.shape[0] // 2
    return jnp.where(first, values[:half], values[half:])


def first_half(rows):
    return lax.broadcasted_iota(jnp.int32, (rows, 128), 1) < HD


def spread_matrix():
    a = lax.broadcasted_iota(jnp.int32, (256, 128), 0) // HD % 2
    b = lax.broadcasted_iota(jnp.int32, (256, 128), 1) // HD
    return jnp.where(a == b, 1.0 / HD, 0.0).astype(BF)


def make_masks(lengths, mask):
    at_row = lax.broadcasted_iota(jnp.int32, (128, 128), 0)
    at_col = lax.broadcasted_iota(jnp.int32, (128, 128), 1)
    for r in range(2):
        end = jnp.int32(0)
        left = jnp.zeros((128, 128), jnp.int32)
        right = jnp.zeros((128, 128), jnp.int32)
        for p in range(4):
            end = end + lengths[r, p]
            left = left + jnp.where(at_row >= end, 1, 0)
            right = right + jnp.where(at_col >= end, 1, 0)
        same = jnp.where(left == right, 1.0, 0.0)
        mask[r, 0:128, :] = same
        mask[r, 128:256, :] = same


def gelu_and_slope(before):
    inner_scale, cubic = 0.7978845608028654, 0.044715
    square = before * before
    tanh = jnp.tanh(inner_scale * before * (1.0 + cubic * square))
    half = 0.5 * (1.0 + tanh)
    slope = half + 0.5 * before * (1.0 - tanh * tanh) * inner_scale * (1.0 + 3.0 * cubic * square)
    return before * half, slope


def gain_rows(gains, layer):
    return tuple(gains[layer, i : i + 1, :] for i in range(6))


class Gather:
    def __init__(self, me, net, w1, wd, nz):
        self.me, self.net, self.w1, self.wd, self.nz = me, net, w1, wd, nz
        self.sibling, self.xs, self.ys, self.zs = me.neighbours()
        self.chunks = [self.chunk(layer, kind) for layer in range(LAYERS) for kind in KINDS]
        every = [(i, k) for i in range(len(self.chunks)) for k in range(7)]
        self.turns = sorted(every, key=lambda turn: (STARTS_AT[turn[0]] + turn[1], turn[0]))
        self.done = 0

    def chunk(self, layer, kind):
        me, w1, wd = self.me, self.w1, self.wd
        down = kind == "down"
        base = 96 * me.c if down else STARTS[kind] + HALF * me.c

        def q(at, k):
            if down:
                return wd.at[layer, :, at, rows16(base + 16 * k, 16), :]
            return w1.at[layer, :, at, :, lanes(base + QUARTER * k, QUARTER)]

        def p(at, k):
            if down:
                return wd.at[layer, k[0], at, rows16(base + 64 + 16 * k[1], 16), :]
            return w1.at[layer, k[0], at, :, lanes(base + C_START + C_WIDTH * k[1], C_WIDTH)]

        def a(at):
            return w1.at[layer, :, at, :, lanes(base + A_START, A_WIDTH)]

        def whole(at):
            if down:
                return wd.at[layer, :, at, rows16(base, 96), :]
            return w1.at[layer, :, at, :, lanes(base, HALF)]

        long = 1 if kind == "up" else -1
        pieces = [(lambda at: q(at, me.y), long), (lambda at: p(at, me.on_x(0)), -long)]
        return SimpleNamespace(
            pieces=pieces, fours=((q, me.on_y, self.ys), (p, me.on_x, self.xs)), whole=whole,
            spare=[] if down else [(a, 1)], norms=layer == 0 and kind == "qkvo", first={}, second=[],
            moving=None, aside=None, norm_moving=[], shared=None,
        )

    def ring(self, pieces, k):
        batch = self.net.batch()
        for view, long in pieces:
            for d in (1, -1):
                if k < 4 or d == long:
                    batch.put(view(PLACES[-d * (k - 1)]), view(PLACES[-d * k]), self.zs[d])
        return batch

    def norm_ring(self, k):
        copies = []
        for d in (1, -1):
            if k < 4 or d == 1:
                block = self.nz.at[(self.me.z - d * (k - 1) + 8) % 8]
                copies.append(self.net.put(block, block, self.zs[d]))
        return copies

    def spread(self, chunk, group):
        batch = self.net.batch()
        for at in GROUPS[group]:
            for view, place, devices in chunk.fours if at is not None else ():
                for d in (1, -1):
                    batch.put(view(at, place(0)), view(at, place(0)), devices[d])
        chunk.first[group] = batch

    def relay(self, chunk, group):
        chunk.first[group].wait_recv()
        batch = self.net.batch()
        for d, at in zip((1, -1), GROUPS[group]):
            for view, place, devices in chunk.fours if at is not None else ():
                block = view(at, place(-d))
                batch.put(block, block, devices[d])
        chunk.second.append(batch)

    def tick(self, chunk, k):
        if 1 <= k <= 4:
            chunk.moving.wait_recv()
            arrive(chunk.norm_moving)
        if k < 4:
            chunk.moving = self.ring(chunk.pieces, k + 1)
            chunk.norm_moving = self.norm_ring(k + 1) if chunk.norms else []
        if k < 5:
            self.spread(chunk, k)
        if 1 <= k <= 5:
            self.relay(chunk, k - 1)
        if chunk.spare and k >= 2:
            if k > 2:
                chunk.aside.wait_recv()
            if k <= 5:
                chunk.aside = self.ring(chunk.spare, k - 1)
        if k == 2:
            chunk.shared = self.net.batch()
        if k >= 2:
            chunk.second[k - 2].wait_recv()
            for at in GROUPS[k - 2]:
                if at is not None:
                    chunk.shared.put(chunk.whole(at), chunk.whole(at), self.sibling)

    def nudge(self):
        if self.done < len(self.turns):
            i, k = self.turns[self.done]
            self.tick(self.chunks[i], k)
            self.done += 1

    def complete(self, i):
        while (i, 6) not in self.turns[: self.done]:
            self.nudge()
        self.nudge()
        if i == len(self.chunks) - 1:
            self.net.settle(len(self.net.sent) - 4)
        self.chunks[i].shared.wait_recv()


STARTS_AT = (0, 0.5, 2.5, 3, 4, 4.5)
GATHER_COPIES = 130
SAVED = ("normed", "unit", "scales", "values", "probs", "mixed", "middle", "second", "hidden", "slope")


def forward_kernel(
    qkv_ref, out_ref, up_ref, wd_ref, norm_ref, tokens, lengths,
    act, w1_out, wd_out, gains, stream_out, *rest,
):
    saved_out, rest = dict(zip(SAVED, rest)), rest[len(SAVED) :]
    kept, rest = dict(zip(SAVED, rest)), rest[len(SAVED) :]
    w1, wd, xf, stream, mask, raw, line, nc, nx, nz, send, recv, local, out_sem, save_sem = rest
    normed, unit, scales, values, probs, mixed, middle, second, hidden, slope = (kept[name] for name in SAVED)
    me = Place()
    x, y, z, c, xl, xh = me.x, me.y, me.z, me.c, me.xl, me.xh
    sibling, xs, ys, zs = me.neighbours()
    met = greet([sibling, xs[1], xs[-1], ys[1], ys[-1], zs[1], zs[-1]])
    net = Net(send, recv, sibling, w1.at[0, 0])

    for i, kind in enumerate(STARTS):
        mine = xf.at[i, :, pl.ds(24 * c, 24), :]
        if kind == "up":
            pltpu.make_async_copy(up_ref.at[:, :, lanes(c * HALF, HALF)], mine, local.at[i]).start()
    nc[c] = jnp.zeros((56, 128), F32)
    line[...] = jnp.zeros((8, 256), F32)
    line[0:2, 0:100] = norm_ref[...].astype(BF).astype(F32)
    first = 100 * lax.axis_index("shard")
    for layer in range(LAYERS):
        row = pltpu.roll(jnp.broadcast_to(line[layer : layer + 1, :], (8, 256)), first % 128, 1)
        for i in range(2):
            nc[c, pl.ds(25 * layer + first // 128 + i, 1), :] = row[0:1, 128 * i : 128 * i + 128]
    own_q, own_h = rows16(16 * y, 16), rows16(64 + 16 * xh, 16)
    own_qd = wd.at[:, xl, PLACES[0], rows16(96 * c + 16 * y, 16), :]
    own_qd[...] = wd_ref[:, own_q, :].astype(BF)
    wd[:, xl, PLACES[0], rows16(96 * c + 64 + 16 * xh, 16), :] = wd_ref[:, own_h, :].astype(BF)
    make_masks(lengths, mask)
    met()
    norm_swap = net.put(nc.at[c], nc.at[c], sibling)
    arrivals = []
    for i, kind in enumerate(STARTS):
        mine = xf.at[i, :, pl.ds(24 * c, 24), :]
        if kind == "up":
            net.put(up_ref.at[:, :, lanes((1 - c) * HALF, HALF)], mine, sibling)
        else:
            at = net.reserve()

            def parts(core):
                if core == 0:
                    return [(qkv_ref.at[:, :, 0:HALF], mine)]
                return [
                    (qkv_ref.at[:, :, HALF : 3 * D], mine.at[:, :, 0:D]),
                    (out_ref, mine.at[:, :, D:HALF]),
                ]

            for core in range(2):

                @pl.when(c == core)
                def _():
                    for src, dst in parts(core):
                        pltpu.make_async_copy(src, dst, local.at[i]).start()
                    for src, dst in parts(1 - core):
                        net.copy(src, dst, sibling, at).start()

            net.sent.append(net.copy(mine, mine, sibling, at))
        arrivals.append((pltpu.make_async_copy(mine, mine, local.at[i]), net.sent[-1]))
    cross = [net.put(own_qd, own_qd, xs[-1])]
    norm_swap.wait_recv()
    nx[xl] = nc[0] + nc[1]
    cross.append(net.put(nx.at[xl], nx.at[xl], xs[1]))
    for i, start in enumerate(STARTS.values()):
        base = start + c * HALF
        arrivals[i][0].wait()
        arrivals[i][1].wait_recv()
        own_q1 = w1.at[:, xl, PLACES[0], :, lanes(base + QUARTER * y, QUARTER)]
        own_a1 = w1.at[:, xl, PLACES[0], :, lanes(base + A_START, A_WIDTH)]
        own_q1[...] = xf[i, :, :, lanes(QUARTER * y, QUARTER)].astype(BF)
        own_a1[...] = xf[i, :, :, A_START : A_START + A_WIDTH].astype(BF)
        cross.append(net.put(own_q1, own_q1, xs[1]))
        cross.append(net.put(own_a1, own_a1, xs[-1]))
        w1[:, xl, PLACES[0], :, lanes(base + C_START + C_WIDTH * xh, C_WIDTH)] = xf[
            i, :, :, lanes(C_START + C_WIDTH * xh, C_WIDTH)
        ].astype(BF)
    arrive(cross)
    nz[z] = nx[0] + nx[1]
    moves = Gather(me, net, w1, wd, nz)
    outs = []

    def out(src, dst, sem):
        outs.append(pltpu.make_async_copy(src, dst, sem))
        outs[-1].start()

    def save(layer, *names):
        for name in names:
            out(kept[name].at[layer], saved_out[name].at[layer], save_sem.at[layer, SAVED.index(name)])

    def wide(layer, start, size):
        cols = lanes(start, size)
        return jnp.concatenate([w1[layer, r, place_of(zb, z), :, cols] for r in range(2) for zb in range(RING)], 0)

    def place_gains():
        total = nz[0]
        for i in range(1, 8):
            total = total + nz[i]
        for layer in range(LAYERS):
            for kind in range(4):
                for k in range(6):
                    at = 25 * layer + 6 * kind + k
                    gains[layer, kind : kind + 1, 128 * k : 128 * k + 128] = total[at : at + 1, :]
            pair = total[25 * layer + 24 : 25 * layer + 25, :]
            turned = pltpu.roll(pair, HD, 1)
            first = first_half(1)
            for kind, both in ((4, jnp.where(first, pair, turned)), (5, jnp.where(first, turned, pair))):
                for k in range(6):
                    gains[layer, kind : kind + 1, 128 * k : 128 * k + 128] = both
            gains[layer, 6:8, :] = jnp.zeros((2, D), F32)

    def forward(layer):
        source = tokens if layer == 0 else stream
        moves.complete(3 * layer)
        out(w1.at[layer, :, :, :, 0 : 4 * D], w1_out.at[layer, :, :, :, 0 : 4 * D], out_sem.at[layer, 0])
        if layer == 0:
            place_gains()
        gain_one, bias_one, gain_two, bias_two, gain_query, gain_key = gain_rows(gains, layer)
        norm_into(normed.at[layer], source, gain_one, bias_one)
        for part in range(3):
            joined = dot(normed[layer], wide(layer, D * part, D))
            if part < 2:
                raw[part] = joined
            else:
                values[layer] = joined.astype(BF)
            moves.nudge()
        save(layer, "normed", "values")
        pair_gains = (gain_query[:, 0:128], gain_key[:, 0:128])
        spread = spread_matrix()
        first_one = first_half(128)

        def attend(p):
            at = pl.ds(p * 128, 128)
            low_parts = []
            for part in range(2):
                whole = raw[part, :, at]
                center = whole - head_mean(whole, spread)
                scale = lax.rsqrt(head_mean(center * center, spread) + eps)
                normal = center * scale
                unit[layer, part, :, at] = normal
                scales[layer, part, :, at] = scale.astype(BF)
                low_parts.append((normal * pair_gains[part]).astype(BF))
            queries, keys = low_parts
            for r in range(2):
                rows = slice(128 * r, 128 * r + 128)
                both = split_heads(queries[rows], first_one)
                scores = dot(both, keys[rows], NT) * HD ** (-0.5)
                scores = jnp.where(mask[r] > 0.5, scores, -1e30)
                exponent = jnp.exp(scores - jnp.max(scores, -1, keepdims=True))
                probability = exponent * (1.0 / jnp.sum(exponent, -1, keepdims=True))
                probs[layer, r, p] = probability
                result = dot(probability.astype(BF), values[layer, rows, at])
                mixed[layer, rows, at] = join_heads(result, first_one).astype(BF)

        for p in range(PAIRS):
            attend(p)
            if p % 2:
                moves.nudge()
        save(layer, "unit", "scales", "probs", "mixed")
        middle[layer] = source[...].astype(F32) + dot(mixed[layer], wide(layer, 3 * D, D))
        norm_into(second.at[layer], middle.at[layer], gain_two, bias_two)
        save(layer, "middle", "second")
        moves.nudge()

        def fourth(t):
            cols = lanes(FOURTH * t, FOURTH)
            raw[0] = dot(second[layer], wide(layer, 4 * D + FOURTH * t, FOURTH))

            def activate(r, carry):
                value, derivative = gelu_and_slope(raw[0, r, :])
                hidden[layer, r, cols] = value.astype(BF)
                slope[layer, r, cols] = derivative.astype(BF)
                return carry

            by_rows(activate)

        moves.complete(3 * layer + 1)
        out(w1.at[layer, :, :, :, 4 * D : 8 * D], w1_out.at[layer, :, :, :, 4 * D : 8 * D], out_sem.at[layer, 3])
        for t in range(4):
            fourth(t)
            moves.nudge()
        save(layer, "hidden", "slope")
        moves.complete(3 * layer + 2)
        for zb in range(RING):
            pltpu.make_async_copy(
                wd.at[layer, :, place_of(zb, z)], wd_out.at[layer, :, zb], out_sem.at[layer, 1]
            ).start()
        outs.append(pltpu.make_async_copy(wd.at[layer], wd_out.at[layer], out_sem.at[layer, 1]))
        whole = jnp.concatenate([wd[layer, r, place_of(zb, z)] for r in range(2) for zb in range(RING)], 0)
        result = middle[layer] + dot(hidden[layer], whole)
        if layer + 1 < LAYERS:
            stream[...] = result
            out(stream, stream_out, out_sem.at[layer, 2])
        else:
            act[...] = result.astype(BF)

    for layer in range(LAYERS):
        forward(layer)
    for copy in outs:
        copy.wait()
    net.finish()


def saved_shapes():
    pair = (2, ROWS, D)
    shapes = {
        "normed": ((ROWS, D), BF), "unit": (pair, F32), "scales": (pair, BF), "values": ((ROWS, D), BF),
        "probs": ((2, PAIRS, 256, 128), F32), "mixed": ((ROWS, D), BF), "middle": ((ROWS, D), F32),
        "second": ((ROWS, D), BF), "hidden": ((ROWS, FF), BF), "slope": ((ROWS, FF), BF),
    }
    return [shapes[name] for name in SAVED]


def forward_pass(qkv, out, up, down, norms, tokens, lengths):
    any_spec, vmem_spec = pl.BlockSpec(memory_space=pl.ANY), pl.BlockSpec(memory_space=pltpu.VMEM)
    smem_spec = pl.BlockSpec(memory_space=pltpu.SMEM)
    saved = [((LAYERS, *shape), kind) for shape, kind in saved_shapes()]
    outs = pl.pallas_call(
        forward_kernel,
        out_shape=(
            jax.ShapeDtypeStruct((ROWS, D), BF),
            jax.ShapeDtypeStruct((LAYERS, 2, RING, BLOCK, WIDE), BF),
            jax.ShapeDtypeStruct((LAYERS, 2, RING, DBLOCK, D), BF),
            jax.ShapeDtypeStruct((LAYERS, 8, D), F32),
            jax.ShapeDtypeStruct((ROWS, D), F32),
            *[jax.ShapeDtypeStruct(*item) for item in saved],
        ),
        in_specs=[any_spec, any_spec, any_spec, vmem_spec, vmem_spec, vmem_spec, smem_spec],
        out_specs=(vmem_spec, any_spec, any_spec, vmem_spec, any_spec, *[any_spec] * len(saved)),
        scratch_shapes=[
            *[pltpu.VMEM(*item) for item in saved],
            pltpu.VMEM((LAYERS, 2, RING, BLOCK, WIDE), BF),
            pltpu.VMEM((LAYERS, 2, RING, DBLOCK, D), BF),
            pltpu.VMEM((2, LAYERS, BLOCK, HALF), F32),
            pltpu.VMEM((ROWS, D), F32),
            pltpu.VMEM((2, 256, 128), F32),
            pltpu.VMEM((2, ROWS, D), F32),
            pltpu.VMEM((8, 256), F32),
            pltpu.VMEM((2, 56, 128), F32),
            pltpu.VMEM((2, 56, 128), F32),
            pltpu.VMEM((8, 56, 128), F32),
            pltpu.SemaphoreType.DMA((GATHER_COPIES,)),
            pltpu.SemaphoreType.DMA((GATHER_COPIES,)),
            pltpu.SemaphoreType.DMA((2,)),
            pltpu.SemaphoreType.DMA((LAYERS, 4)),
            pltpu.SemaphoreType.DMA((LAYERS, len(SAVED))),
        ],
        compiler_params=pltpu.CompilerParams(
            collective_id=0, has_side_effects=True, vmem_limit_bytes=63 * 1024 * 1024
        ),
        name="gather_and_forward",
    )(qkv, out, up, down, norms, tokens, lengths)
    return outs[0], outs[1], outs[2], outs[3], outs[4], outs[5:]


HALVES = (slice(4, 8), slice(0, 4))
PARTS = tuple((slice(7 - i, 8 - i), slice(i, i + 1)) for i in range(4))
SCATTER_COPIES = 150
SUM_ORDER = tuple((layer, kind) for layer in (1, 0) for kind in ("down", "up", "qkvo"))


class Scatter:
    def __init__(self, me, net, grads, buffers, sems):
        self.me, self.net, self.grads, self.b = me, net, grads, buffers
        self.local, self.swap_send, self.swap_recv, self.credit = sems
        self.sibling, self.xs, self.ys, self.zs = me.neighbours()
        self.chunks = [self.chunk(i, layer, kind) for i, (layer, kind) in enumerate(SUM_ORDER)]
        self.kept, self.swapped, self.turns = [], [], 0

    def chunk(self, index, layer, kind):
        me, b, down = self.me, self.b, kind == "down"
        own = b["own_" + kind]

        def q(at, k):
            if down:
                return own.at[layer, :, at, rows16(16 * k, 16), :]
            return own.at[layer, :, at, :, lanes(QUARTER * k, QUARTER)]

        def p(at, k):
            if down:
                return own.at[layer, k[0], at, rows16(64 + 16 * k[1], 16), :]
            return own.at[layer, k[0], at, :, lanes(C_START + C_WIDTH * k[1], C_WIDTH)]

        def a(at):
            return own.at[layer, :, at, :, A_START : A_START + A_WIDTH]

        def q_buffer(name):
            return lambda at: b[name + kind].at[layer, :, at]

        def p_buffer(name):
            return lambda at: b[name + kind].at[layer, at]

        def z_pair(name):
            return {1: (b["zp" + name + kind], layer), -1: (b["zm" + name + kind], layer)}

        fours = [
            (q, me.on_y, self.ys, *[q_buffer(name) for name in ("yf_", "yp_", "ym_")]),
            (p, me.on_x, self.xs, *[p_buffer(name) for name in ("xf_", "xp_", "xm_")]),
        ]
        long = 1 if kind == "up" else -1
        chain = [
            (lambda at: q(at, me.y), long, z_pair("q_")),
            (lambda at: p(at, me.on_x(0)), -long, z_pair("p_")),
        ]
        spare = [] if down else [(a, 1, z_pair("a_"))]
        return SimpleNamespace(
            index=index, layer=layer, kind=kind, fours=fours, chain=chain, spare=spare,
            far={}, second={}, near=None, moving=None, aside=None, at=0, ready=False,
        )

    def mine_and_theirs(self, chunk):
        return self.b["own_" + chunk.kind].at[chunk.layer], self.b["sib_" + chunk.kind]

    def swap_copy(self, chunk, src, dst):
        i = chunk.index
        return pltpu.make_async_remote_copy(
            src, dst, self.swap_send.at[i], self.swap_recv.at[i], device_id=self.sibling, device_id_type=MESH
        )

    def load(self, chunk):
        layer, c, kind = chunk.layer, self.me.c, chunk.kind
        mine, theirs = self.mine_and_theirs(chunk)
        sem = self.local.at[chunk.index]
        if kind != "qkvo":
            grad = self.grads[kind][layer]

            def half(core):
                if kind == "down":
                    return grad.at[:, :, rows16(96 * core, 96), :]
                return grad.at[:, :, :, lanes(HALF * core, HALF)]

            pltpu.make_async_copy(half(c), mine, sem).start()
            self.swap_copy(chunk, half(1 - c), theirs).start()
            return
        qkv, out = (self.grads[name][layer] for name in ("qkv", "out"))

        def parts(core, to):
            if core == 0:
                return [(qkv.at[:, :, :, 0:HALF], to)]
            return [(qkv.at[:, :, :, HALF : 3 * D], to.at[:, :, :, 0:D]), (out, to.at[:, :, :, D:HALF])]

        for core in range(2):

            @pl.when(c == core)
            def _():
                for src, dst in parts(core, mine):
                    pltpu.make_async_copy(src, dst, sem).start()
                for src, dst in parts(1 - core, theirs):
                    self.swap_copy(chunk, src, dst).start()

    def loaded(self, chunk):
        mine, theirs = self.mine_and_theirs(chunk)
        pltpu.make_async_copy(mine, mine, self.local.at[chunk.index]).wait()
        self.swap_copy(chunk, mine, theirs).wait_recv()

        def add(i, carry):
            for rows in range(2):
                mine[rows, i] = mine[rows, i] + theirs[rows, i]
            return carry

        lax.fori_loop(0, RING, add, 0)

    @staticmethod
    def sum_into(ref, *others):
        total = ref[...]
        for other in others:
            total = total + other[...]
        ref[...] = total

    def four_far(self, chunk, part):
        chunk.far[part] = self.net.batch()
        for d, at in zip((1, -1), PARTS[part]):
            for view, k, devices, first, ahead, behind in chunk.fours:
                chunk.far[part].put(view(at, k(2)), first(at), devices[d])

    def four_near(self, chunk):
        chunk.near = self.net.batch()
        for d, at in zip((1, -1), HALVES):
            for view, k, devices, first, ahead, behind in chunk.fours:
                back = ahead if d == -1 else behind
                chunk.near.put(view(at, k(-d)), back(at), devices[-d])

    def four_second(self, chunk, part):
        chunk.far[part].wait_recv()
        chunk.second[part] = self.net.batch()
        for d, at in zip((1, -1), PARTS[part]):
            for view, k, devices, first, ahead, behind in chunk.fours:
                block, front = view(at, k(d)), ahead if d == 1 else behind
                self.sum_into(block, first(at))
                chunk.second[part].put(block, front(at), devices[d])

    def four_last(self, chunk, part):
        if part == 0:
            chunk.near.wait_recv()
        chunk.second[part].wait_recv()
        for at in PARTS[part]:
            for view, k, devices, first, ahead, behind in chunk.fours:
                self.sum_into(view(at, k(0)), ahead(at), behind(at))

    def chain_step(self, pieces, k, before):
        if before:
            before.wait_recv()
        batch = self.net.batch()
        for view, long, buffers in pieces:
            for d in (1, -1):
                if k == 1 and d != long:
                    continue
                block = view(PLACES[d * (5 - k)])
                buffer, layer = buffers[d]
                if k > 2 or k == 2 and d == long:
                    self.sum_into(block, buffer.at[k - 2, layer])
                batch.put(block, buffer.at[k - 1, layer], self.zs[d])
        return batch

    def chain_last(self, pieces, before):
        before.wait_recv()
        for view, long, buffers in pieces:
            self.sum_into(view(PLACES[0]), *[buffers[d][0].at[3, buffers[d][1]] for d in (1, -1)])

    def begin(self, i):
        chunk = self.chunks[i]
        if chunk.layer == 0:
            while self.chunks[i - 3].at < 1:
                self.tick(self.chunks[i - 3])
            pl.semaphore_wait(self.credit.at[KINDS.index(chunk.kind)], 1)
        self.load(chunk)
        chunk.ready, chunk.begun = True, self.turns

    def tick(self, chunk):
        t = chunk.at
        chunk.at += 1
        if t > 6:
            self.to_copies(chunk) if t == 7 else self.to_sibling(chunk)
            return
        if t == 0:
            self.loaded(chunk)
            if chunk.layer == 1:
                pl.semaphore_signal(
                    self.credit.at[KINDS.index(chunk.kind)], inc=1, device_id=self.sibling, device_id_type=MESH
                )
        if t < 4:
            self.four_far(chunk, t)
        if t == 0:
            self.four_near(chunk)
        if 1 <= t <= 4:
            self.four_second(chunk, t - 1)
        if 2 <= t <= 5:
            self.four_last(chunk, t - 2)
        if 2 <= t < 6:
            chunk.moving = self.chain_step(chunk.chain, t - 1, chunk.moving)
        if t < 4 and chunk.spare:
            chunk.aside = self.chain_step(chunk.spare, t + 1, chunk.aside)
        if t == 6:
            if chunk.spare:
                self.chain_last(chunk.spare, chunk.aside)
            self.chain_last(chunk.chain, chunk.moving)
            self.over_copies(chunk)

    def slots(self, chunk, name):
        return self.b[name + chunk.kind].at[chunk.layer]

    @staticmethod
    def sum_slots(slots):
        total = slots[0].astype(F32)
        for i in range(1, 4):
            total = total + slots[i].astype(F32)
        return total.astype(BF)

    def over_copies(self, chunk):
        me, net, layer, down = self.me, self.net, chunk.layer, chunk.kind == "down"
        x, y, z, xl, xh = me.x, me.y, PLACES[0], me.xl, me.xh
        own = self.b["own_" + chunk.kind]

        def part_q(k):
            if down:
                return own.at[layer, k, z, rows16(16 * y, 16), :]
            return own.at[layer, k, z, :, lanes(QUARTER * y, QUARTER)]

        def part_a(k):
            return own.at[layer, k, z, :, A_START : A_START + A_WIDTH]

        over_x, over_y = net.batch(), net.batch()
        for view, name in ((part_q, "xs_"), (part_a, "xa_"))[: 1 if down else 2]:
            slots = self.slots(chunk, name)
            for d in (1, -1, 2):
                over_x.put(view(xl if d == 2 else 1 - xl), slots.at[x], self.xs[d])
            slots[x] = view(xl)[...]
        if down:
            part_p = own.at[layer, xl, z, rows16(64 + 16 * xh, 16), :]
        else:
            part_p = own.at[layer, xl, z, :, lanes(C_START + C_WIDTH * xh, C_WIDTH)]
        slots = self.slots(chunk, "ys_")
        for d in (1, -1, 2):
            over_y.put(part_p, slots.at[y], self.ys[d])
        slots[y] = part_p[...]
        chunk.over = (over_x, over_y)

    def to_copies(self, chunk):
        me, net, down = self.me, self.net, chunk.kind == "down"
        x, y, xh = me.x, me.y, me.xh
        total = self.b["out_down" if down else "rb_" + chunk.kind].at[chunk.layer]
        over_x, over_y = chunk.over
        last = net.batch()
        over_x.wait_recv()
        if not down:
            slots = self.slots(chunk, "ya_")
            slots[y] = self.sum_slots(self.slots(chunk, "xa_"))
            for d in (1, -1, 2):
                last.put(slots.at[y], slots.at[y], self.ys[d])
        mine = total.at[rows16(16 * y, 16), :] if down else total.at[:, lanes(QUARTER * y, QUARTER)]
        mine[...] = self.sum_slots(self.slots(chunk, "xs_"))
        for d in (1, -1, 2):
            last.put(mine, mine, self.ys[d])
        over_y.wait_recv()
        if down:
            mine = total.at[rows16(64 + 16 * xh, 16), :]
        else:
            mine = total.at[:, lanes(C_START + C_WIDTH * xh, C_WIDTH)]
        mine[...] = self.sum_slots(self.slots(chunk, "ys_"))
        last.put(mine, mine, self.xs[2])
        chunk.last = last

    def to_sibling(self, chunk):
        chunk.last.wait_recv()
        kind, layer, c = chunk.kind, chunk.layer, self.me.c
        if kind == "down":
            return
        total, wide = self.b["rb_" + kind].at[layer], self.b["rf_" + kind].at[layer]
        total[:, A_START : A_START + A_WIDTH] = self.sum_slots(self.slots(chunk, "ya_"))
        wide[...] = total[...].astype(F32)
        target = self.b["out_wide"].at[layer, :, lanes(STARTS[kind] + c * HALF, HALF)]
        self.swapped.append(self.net.put(wide.at[pl.ds(24 * (1 - c), 24), :], target, self.sibling))
        keep = pltpu.make_async_copy(wide.at[pl.ds(24 * c, 24), :], target, self.local.at[6 + len(self.kept)])
        keep.start()
        self.kept.append(keep)

    def turn(self, rest=None):
        self.turns += 1
        rest = GAP if rest is None else rest
        open_chunks = [ch for ch in self.chunks if ch.ready and ch.at < 9]
        rested = [ch for ch in open_chunks if self.turns - ch.begun >= (rest if ch.at else rest and REST)]
        for chunk in sorted(rested, key=lambda ch: SUM_AFTER[ch.index] + ch.at)[:AT_ONCE]:
            chunk.begun = self.turns
            self.tick(chunk)
        return bool(open_chunks)

    def swaps_sent(self):
        for chunk in self.chunks:
            self.swap_copy(chunk, *self.mine_and_theirs(chunk)).wait_send()


SUM_AFTER = (0, 2, 4, 6, 8, 10)
REST = 4
GAP = 3
AT_ONCE = 5


def buffer_shapes():
    shapes = {}
    for kind in KINDS:
        rows, cols = (96, D) if kind == "down" else (BLOCK, HALF)
        quarter = (16, D) if kind == "down" else (BLOCK, QUARTER)
        half = (16, D) if kind == "down" else (BLOCK, C_WIDTH)
        shapes["own_" + kind] = (2, 2, RING, rows, cols)
        shapes["sib_" + kind] = (2, RING, rows, cols)
        for name in ("yf_", "yp_", "ym_"):
            shapes[name + kind] = (2, 2, RING, *quarter)
        for name in ("xf_", "xp_", "xm_"):
            shapes[name + kind] = (2, RING, *half)
        for name in ("zp", "zm"):
            shapes[name + "q_" + kind] = (4, 2, 2, *quarter)
            shapes[name + "p_" + kind] = (4, 2, *half)
        shapes["xs_" + kind] = (2, 4, *quarter)
        shapes["ys_" + kind] = (2, 4, *half)
        if kind != "down":
            for name in ("zp", "zm"):
                shapes[name + "a_" + kind] = (4, 2, 2, BLOCK, A_WIDTH)
            shapes["xa_" + kind] = shapes["ya_" + kind] = (2, 4, BLOCK, A_WIDTH)
            shapes["rb_" + kind] = (2, BLOCK, HALF)
    return shapes


BUFFERS = buffer_shapes()
WEIGHT_SLOTS = 3
STAGE_SLOTS = 2
GRAD_SHAPES = {"qkv": (D, 3 * D), "out": (D, D), "up": (D, FF), "down": (FF, D)}


def backward_kernel(tokens, cotangent, gains, w1_ref, wd_ref, stream_ref, *rest):
    saved, rest = dict(zip(SAVED, rest)), rest[len(SAVED) :]
    input_grad, out1, outd, outn = rest[:4]
    grads_flat, rest = rest[4:12], rest[12:]
    names = tuple(GRAD_SHAPES)
    grads = {name: grads_flat[2 * i : 2 * i + 2] for i, name in enumerate(names)}
    kept, rest = dict(zip(SAVED, rest)), rest[len(SAVED) :]
    b, rest = dict(zip(BUFFERS, rest)), rest[len(BUFFERS) :]
    (
        rf, stream, weight, low, wide_low, grad, slow, turned, stage, gn, norm_sum, nc, nz, ny, nx,
        send, recv, local, swap_send, swap_recv, credit, load_sem, weight_sem, store_sem, plain_sem,
    ) = rest
    unit, scales, values, probs = (kept[name] for name in ("unit", "scales", "values", "probs"))
    me = Place()
    x, y, z, c, xl, xh = me.x, me.y, me.z, me.c, me.xl, me.xh
    sibling, xs, ys, zs = me.neighbours()

    met = greet([sibling, *xs.values(), *ys.values(), *zs.values()])
    use_order = ("hidden", "slope", "second", "middle", "mixed", "probs", "values", "unit", "scales", "normed")
    fetched = {}

    def fetch(layer, *wanted):
        for name in wanted:
            fetched[name] = pltpu.make_async_copy(
                saved[name].at[layer], kept[name], load_sem.at[SAVED.index(name)]
            )
            fetched[name].start()

    wide_weight = weight.reshape(WEIGHT_SLOTS, 2, RING, BLOCK, D)
    tall_weight = weight.reshape(WEIGHT_SLOTS, 4, DBLOCK, D)
    weight_views = []
    for layer in reversed(range(LAYERS)):
        for t in range(4):
            weight_views.append((wd_ref.at[layer, t // 2, t % 2 * 4 : t % 2 * 4 + 4], tall_weight))
        for start in (*[4 * D + FOURTH * t for t in range(4)], 3 * D, 0, D, 2 * D):
            weight_views.append((w1_ref.at[layer, :, :, :, start : start + D], wide_weight))
    weight_copies = []

    def ask_weight():
        n = len(weight_copies)
        if n < len(weight_views):
            slot = n % WEIGHT_SLOTS
            view, to = weight_views[n]
            weight_copies.append(pltpu.make_async_copy(view, to.at[slot], weight_sem.at[slot]))
            weight_copies[-1].start()

    taken = []

    def take_weight():
        n = len(taken)
        taken.append(n)
        weight_copies[n].wait()
        slot = n % WEIGHT_SLOTS
        if weight_views[n][1] is tall_weight:
            return weight[slot]
        return jnp.concatenate(
            [wide_weight[slot, r, place_of(zb, z)] for r in range(2) for zb in range(RING)], 0
        )

    first_copies = [
        pltpu.make_async_copy(cotangent, low, plain_sem.at[0]),
        pltpu.make_async_copy(stream_ref, stream, plain_sem.at[1]),
    ]
    first_copies[0].start()
    ask_weight()
    fetch(1, *use_order[:2])
    for i in range(WEIGHT_SLOTS - 1):
        ask_weight()
    fetch(1, *use_order[2:])
    first_copies[1].start()

    net = Net(send, recv, sibling, b["own_qkvo"].at[0, 0])
    shaped = {name: grads[name] for name in names}
    b.update(out_down=outd, out_wide=out1, rf_qkvo=rf.at[0], rf_up=rf.at[1])
    sums = Scatter(me, net, shaped, b, (local, swap_send, swap_recv, credit))

    pending = {}
    count = [0]

    def flush():
        for copy in pending.values():
            copy.wait()
        pending.clear()

    def emit(value, name, layer, start, by_row):
        slot = count[0] % STAGE_SLOTS
        count[0] += 1
        if slot in pending:
            pending.pop(slot).wait()
        target, low_value = grads[name][layer], value.astype(BF)
        whole = stage.at[slot]
        if by_row:
            stage[slot] = low_value
            for i in range(4):
                row = start // DBLOCK + i
                pltpu.make_async_copy(
                    stage.at[slot, DBLOCK * i : DBLOCK * i + DBLOCK],
                    target.at[row // RING, place_of(row % RING, z)],
                    store_sem.at[slot],
                ).start()
            pending[slot] = pltpu.make_async_copy(whole, whole, store_sem.at[slot])
            return
        src = stage.at[slot].reshape(2, RING, BLOCK, D)
        for row in range(2 * RING):
            src[row // RING, place_of(row % RING, z)] = low_value[BLOCK * row : BLOCK * row + BLOCK]
        pending[slot] = pltpu.make_async_copy(src, target.at[:, :, :, start : start + D], store_sem.at[slot])
        pending[slot].start()

    def put_rows(layer, kind, rows):
        for i, row in enumerate(rows):
            for k in range(6):
                at = 25 * layer + 6 * (kind + i) + k
                gn[at : at + 1, :] = row[:, 128 * k : 128 * k + 128]

    def backward(layer):
        again = layer > 0
        gain_one, bias_one, gain_two, bias_two, gain_query, gain_key = gain_rows(gains, layer)
        slope, hidden = kept["slope"], kept["hidden"]
        fetched["hidden"].wait()
        fetched["slope"].wait()
        for t in range(4):
            cols = slice(FOURTH * t, FOURTH * t + FOURTH)
            grad_hidden = dot(low[...], take_weight(), NT)
            wide_low[:, cols] = (slope[:, cols].astype(F32) * grad_hidden).astype(BF)
            ask_weight()
            turned[...] = hidden[:, cols].T
            emit(dot(turned[...], low[...]), "down", layer, FOURTH * t, True)
            sums.turn()
        fetched["second"].wait()
        turned[...] = kept["second"][...].T
        if again:
            fetch(layer - 1, "slope", "hidden", "second")
        for t in range(4):
            cols = slice(FOURTH * t, FOURTH * t + FOURTH)
            part = dot(wide_low[:, cols], take_weight(), NT)
            slow[...] = part if t == 0 else slow[...] + part
            ask_weight()
            if t == 0:
                flush()
                if layer == 1:
                    met()
                sums.begin(0 if layer == 1 else 3)
            emit(dot(turned[...], wide_low[:, cols]), "up", layer, FOURTH * t, False)
            sums.turn()
        flush()
        sums.begin(1 if layer == 1 else 4)
        fetched["middle"].wait()
        put_rows(layer, 2, norm_back(kept["middle"], slow, gain_two, grad, low))
        fetched["mixed"].wait()
        turned[...] = kept["mixed"][...].T
        if again:
            fetch(layer - 1, "middle", "mixed")
        emit(dot(turned[...], low[...]), "out", layer, 0, False)
        wide_low[:, 3 * D : 4 * D] = dot(low[...], take_weight(), NT).astype(BF)
        ask_weight()
        sums.turn()
        for name in ("probs", "values", "unit", "scales"):
            fetched[name].wait()
        pair_gains = (gain_query[:, 0:128], gain_key[:, 0:128])
        spread = spread_matrix()
        first_one = first_half(128)

        def attend(p, carry):
            at = pl.ds(p * 128, 128)
            normals = [unit[part, :, at] for part in range(2)]
            queries, keys = ((normals[part] * pair_gains[part]).astype(BF) for part in range(2))
            slopes = ([], [])
            for r in range(2):
                rows = slice(128 * r, 128 * r + 128)
                both = split_heads(queries[rows], first_one)
                grad_both = split_heads(wide_low[rows, pl.ds(3 * D + p * 128, 128)], first_one)
                probability = probs[r, p]
                grad_values = dot(probability.astype(BF), grad_both, TN)
                wide_low[rows, pl.ds(2 * D + p * 128, 128)] = grad_values.astype(BF)
                grad_probs = dot(grad_both, values[rows, at], NT)
                weighted = grad_probs * probability
                inner = jnp.sum(weighted, -1, keepdims=True)
                grad_scores = (weighted - probability * inner).astype(BF)
                slopes[0].append(join_heads(dot(grad_scores, keys[rows]), first_one) * HD ** (-0.5))
                slopes[1].append(dot(grad_scores, both, TN) * HD ** (-0.5))
            sums_now = []
            for part in range(2):
                up = jnp.concatenate(slopes[part], 0)
                normal = normals[part]
                sums_now.append(carry[part] + fold(up * normal))
                inner = up * pair_gains[part]
                along = head_mean(inner * normal, spread)
                result = scales[part, :, at].astype(F32) * (inner - head_mean(inner, spread) - normal * along)
                wide_low[:, pl.ds(part * D + p * 128, 128)] = result.astype(BF)
            return tuple(sums_now)

        zero = jnp.zeros((8, 128), F32)
        head_sums = (zero, zero)
        for p in range(PAIRS):
            head_sums = attend(p, head_sums)
            if p % 2:
                sums.turn()
        totals = []
        for part in head_sums:
            total = jnp.sum(part, 0, keepdims=True)
            totals.append(total + pltpu.roll(total, HD, 1))
        gn[25 * layer + 24 : 25 * layer + 25, :] = jnp.where(first_half(1), *totals)
        if again:
            fetch(layer - 1, "probs", "values", "unit", "scales")
        fetched["normed"].wait()
        turned[...] = kept["normed"][...].T
        if again:
            fetch(layer - 1, "normed")
        for part in range(3):
            cols = slice(D * part, D * part + D)
            emit(dot(turned[...], wide_low[:, cols]), "qkv", layer, D * part, False)
            sums.turn()
        flush()
        sums.begin(2 if layer == 1 else 5)
        for part in range(3):
            cols = slice(D * part, D * part + D)
            piece = dot(wide_low[:, cols], take_weight(), NT)
            slow[...] = piece if part == 0 else slow[...] + piece
            ask_weight()
        if layer == 1:
            first_copies[1].wait()
        put_rows(layer, 0, norm_back(stream if layer == 1 else tokens, slow, gain_one, grad, low))

    first_copies[0].wait()

    def turn(r, carry):
        grad[r, :] = low[r, :].astype(F32)
        return carry

    by_rows(turn)
    gn[...] = jnp.zeros(gn.shape, F32)
    for layer in reversed(range(LAYERS)):
        backward(layer)
    grad_out = pltpu.make_async_copy(low, input_grad, plain_sem.at[0])
    grad_out.start()

    nc[c] = gn[...]
    norm_swap = net.put(gn, nc.at[c], sibling)
    norm_moving = [norm_swap]

    def norm_ring(k):
        copies = []
        for d in (1, -1):
            if k < 4 or d == 1:
                slot = nz.at[(z - d * (k - 1) + 8) % 8]
                copies.append(net.put(slot, slot, zs[d]))
        return copies

    t = 0
    while sums.turn(0) or t < 7:
        if sums.chunks[-2].at > 8:
            net.settle(20)
        arrive(norm_moving)
        norm_moving = []
        if t == 0:
            nz[z] = nc[0] + nc[1]
        if t < 4:
            norm_moving = norm_ring(t + 1)
        elif t == 4:
            total = nz[0]
            for i in range(1, 8):
                total = total + nz[i]
            ny[y] = total
            norm_moving = [net.put(ny.at[y], ny.at[y], ys[d]) for d in (1, -1, 2)]
        elif t == 5:
            nx[x] = ny[0] + ny[1] + ny[2] + ny[3]
            norm_moving = [net.put(nx.at[x], nx.at[x], xs[d]) for d in (1, -1, 2)]
        elif t == 6:
            norm_sum[0:56, :] = nx[0] + nx[1] + nx[2] + nx[3]
        t += 1

    arrive(sums.swapped)
    shard = lax.axis_index("shard")
    for row, (layer, first) in enumerate(((0, 100 * shard), (1, 100 * shard), (0, 3 * D + 24 * shard), (1, 3 * D + 24 * shard))):
        at = 25 * layer + first // 128
        pair = [jnp.broadcast_to(norm_sum[pl.ds(at + i, 1), :], (8, 128)) for i in range(2)]
        turned_row = pltpu.roll(jnp.concatenate(pair, 1), (256 - first % 128) % 256, 1)
        outn[row : row + 1, :] = turned_row[0:1, 0:128]
    outn[4:8, :] = jnp.zeros((4, 128), F32)
    for copy in sums.kept:
        copy.wait()
    grad_out.wait()
    net.finish()
    sums.swaps_sent()


def backward_pass(tokens, cotangent, gains, w1, wd, stream, saved):
    any_spec, vmem_spec = pl.BlockSpec(memory_space=pl.ANY), pl.BlockSpec(memory_space=pltpu.VMEM)
    grad_shapes = [
        (2, RING, shape[0] // 16, shape[1]) for shape in GRAD_SHAPES.values() for layer in range(LAYERS)
    ]
    outs = pl.pallas_call(
        backward_kernel,
        out_shape=(
            jax.ShapeDtypeStruct((ROWS, D), BF),
            jax.ShapeDtypeStruct((LAYERS, 24, WIDE), F32),
            jax.ShapeDtypeStruct((LAYERS, 96, D), BF),
            jax.ShapeDtypeStruct((8, 128), F32),
            *[jax.ShapeDtypeStruct(shape, BF) for shape in grad_shapes],
        ),
        in_specs=[vmem_spec, any_spec, vmem_spec, any_spec, any_spec, any_spec, *[any_spec] * len(SAVED)],
        out_specs=(any_spec, any_spec, vmem_spec, vmem_spec, *[any_spec] * len(grad_shapes)),
        scratch_shapes=[
            *[pltpu.VMEM(*item) for item in saved_shapes()],
            *[pltpu.VMEM(shape, BF) for shape in BUFFERS.values()],
            pltpu.VMEM((2, 2, BLOCK, HALF), F32),
            pltpu.VMEM((ROWS, D), F32),
            pltpu.VMEM((WEIGHT_SLOTS, D, D), BF),
            pltpu.VMEM((ROWS, D), BF),
            pltpu.VMEM((ROWS, FF), BF),
            pltpu.VMEM((ROWS, D), F32),
            pltpu.VMEM((ROWS, D), F32),
            pltpu.VMEM((D, ROWS), BF),
            pltpu.VMEM((STAGE_SLOTS, D, D), BF),
            pltpu.VMEM((56, 128), F32),
            pltpu.VMEM((64, 128), F32),
            pltpu.VMEM((2, 56, 128), F32),
            pltpu.VMEM((8, 56, 128), F32),
            pltpu.VMEM((4, 56, 128), F32),
            pltpu.VMEM((4, 56, 128), F32),
            pltpu.SemaphoreType.DMA((SCATTER_COPIES,)),
            pltpu.SemaphoreType.DMA((SCATTER_COPIES,)),
            pltpu.SemaphoreType.DMA((10,)),
            pltpu.SemaphoreType.DMA((6,)),
            pltpu.SemaphoreType.DMA((6,)),
            pltpu.SemaphoreType.REGULAR((3,)),
            pltpu.SemaphoreType.DMA((len(SAVED),)),
            pltpu.SemaphoreType.DMA((WEIGHT_SLOTS,)),
            pltpu.SemaphoreType.DMA((STAGE_SLOTS,)),
            pltpu.SemaphoreType.DMA((2,)),
        ],
        compiler_params=pltpu.CompilerParams(
            collective_id=1, has_side_effects=True, vmem_limit_bytes=63 * 1024 * 1024
        ),
        name="backward_and_scatter",
    )(tokens, cotangent, gains, w1, wd, stream, *saved)
    return outs[:4]


STEPS = 3
FACTOR = 65536 ** (-0.5)


def updated(gradient_sum, master, moment, average):
    gradient_scaled = gradient_sum * FACTOR
    moment_new = momentum_decay * moment + gradient_scaled
    master_new = master - learn_rate * (gradient_scaled + momentum_decay * moment_new)
    average_new = average_decay * average + (1.0 - average_decay) * master_new
    return master_new, moment_new, average_new, master_new.astype(BF)


def update_kernel(*refs):
    ins, outs = refs[:22], refs[22:]
    for i in range(5):
        sums, old, new = ins[4 * i], ins[4 * i + 1 : 4 * i + 4], outs[4 * i : 4 * i + 4]
        total = sums[0:2, 0:100] if i == 4 else sums[...].astype(F32)
        for ref, value in zip(new, updated(total, *[ref[...] for ref in old])):
            ref[...] = value
    for i in range(2):
        outs[20 + i][...] = ins[20 + i][...]
    outs[22][...] = ins[16][2:4, 0:24] * FACTOR


def update(sums, states, rows):
    in_specs, out_specs, shapes, args = [], [], [], []
    starts = (0, 3 * D, 4 * D, 0, 0)
    for start, total, state in zip(starts, sums, states):
        shape = state[0].shape
        if len(shape) == 2:
            block, place = shape, lambda i: (0, 0)
            total_block, total_place = total.shape, place
        elif shape[1] == 96:
            block, place = (shape[0], shape[1] // STEPS, shape[2]), lambda i: (0, i, 0)
            total_block, total_place = block, place
        else:
            block, place = (*shape[:2], shape[2] // STEPS), lambda i: (0, 0, i)
            total_block, total_place = block, lambda i, first=start // (shape[2] // STEPS): (0, 0, first + i)
        spec = pl.BlockSpec(block, place)
        in_specs += [pl.BlockSpec(total_block, total_place), spec, spec, spec]
        out_specs += [spec] * 4
        shapes += [jax.ShapeDtypeStruct(shape, kind) for kind in (F32, F32, F32, BF)]
        args += [total, *state]
    row_spec = pl.BlockSpec((ROWS, D // STEPS), lambda i: (0, i))
    shift = (LAYERS, 24)
    return pl.pallas_call(
        update_kernel,
        grid=(STEPS,),
        out_shape=[*shapes, *[jax.ShapeDtypeStruct((ROWS, D), BF)] * 2, jax.ShapeDtypeStruct(shift, F32)],
        in_specs=[*in_specs, row_spec, row_spec],
        out_specs=[*out_specs, row_spec, row_spec, pl.BlockSpec(shift, lambda i: (0, 0))],
        compiler_params=pltpu.CompilerParams(vmem_limit_bytes=63 * 1024 * 1024),
        name="update",
    )(*args, *rows)


def body(
    tokens, cotangent, picture_lengths, w_qkv, mom_qkv, ema_qkv, w_out, mom_out, ema_out, w_up, mom_up, ema_up,
    w_down, mom_down, ema_down, norms, mom_norms, ema_norms,
):
    flat_tokens = tokens.reshape(ROWS, D)
    act, w1, wd, gains, stream, saved = forward_pass(
        w_qkv, w_out, w_up, w_down, norms, flat_tokens, picture_lengths.reshape(2, 4)
    )
    input_grad, sum1, sumd, sumn = backward_pass(
        flat_tokens, cotangent.reshape(ROWS, D), gains, w1, wd, stream, saved
    )
    outs = update(
        (sum1, sum1, sum1, sumd, sumn),
        (
            (w_qkv, mom_qkv, ema_qkv), (w_out, mom_out, ema_out), (w_up, mom_up, ema_up),
            (w_down, mom_down, ema_down), (norms, mom_norms, ema_norms),
        ),
        (act, input_grad),
    )
    return (outs[20].reshape(tokens.shape), outs[21].reshape(tokens.shape), *outs[:20], outs[22])


def solution(mesh):
    rows = P(None, ("shard", "rep"), None, None)
    wide, flat = P(None, "shard", None), P(None, "shard")
    return jax.shard_map(
        body,
        mesh=mesh,
        in_specs=(rows, rows, P(None, ("shard", "rep"), None), *[wide] * 12, *[flat] * 3),
        out_specs=(rows, rows, *[wide] * 16, *[flat] * 5),
        check_vma=False,
    )
```

time: 849 us -> 218 us (0.26)
  waiting for transfers between devices: 312 us -> 0 us
  Pallas kernels: 0 us -> 214 us
  blocking collectives: 163 us -> 0 us
  matrix products: 137 us -> 0 us
  local copies, waits for them, and re-layouts: 136 us -> 0 us
  other arithmetic: 72.7 us -> 0 us
  between operations: 18.7 us -> 1.14 us
    pallas_call x0 -> x3, Pallas kernels: none -> 214 us  [the longest x1 112 us: backward_pass(): pl.pallas_call(backward_kernel, out_shape=(jax.ShapeDtypeStruct((ROWS, D)...]
    dot_general x72 -> x0, matrix products: 137 us -> none  [the longest x4 20.5 us: backward_layer(): grad_up = jnp.dot(second.T, grad_before, preferred_element_type=jnp.float32)]
    all_gather x2 -> x0, waiting for transfers between devices: 118 us -> none  [the longest x1 69.5 us: in_one_piece(): lax.all_gather(both, axis, axis=dim, tiled=True)]
    unnamed x386 -> x0, local copies, waits for them, and re-layouts: 115 us -> none
    reduce_scatter x1 -> x0, waiting for transfers between devices: 103 us -> none  [body(): lax.psum_scatter(summed[3].astype(jnp.bfloat16), 'shard', scatter_dimensi...]
    unnamed x1 -> x0, blocking collectives: 103 us -> none
    psum x1 -> x0, waiting for transfers between devices: 90.6 us -> none  [body(): lax.psum(as_sent(shares), 'rep')]
    convert_element_type x23 -> x0, other arithmetic: 43.3 us -> none  [the longest x1 10.6 us: body(): summed[2].astype(jnp.bfloat16)]
  transfers between devices with their start and end apart: 5 -> 0, of which waited for: 4 -> 0; matrix products, arithmetic and copies ran while one was open for 9% -> 0% of each run, Pallas kernels for 0% -> 0%
where the time goes in v1:
time: 218 us; the launch traced here: 215 us
  Pallas kernels  214 us (98%)
    pallas_call x1, Pallas kernels, backward_pass(): pl.pallas_call(backward_kernel, out_shape=(jax.ShapeDtypeStruct((ROWS, D)...  112 us
    pallas_call x1, Pallas kernels, forward_pass(): pl.pallas_call(forward_kernel, out_shape=(jax.ShapeDtypeStruct((ROWS, D),...  94.6 us
    pallas_call x1, Pallas kernels, update(): pl.pallas_call(update_kernel, grid=(STEPS,), out_shape=[*shapes, *[jax.Sh...  7.11 us

profile of v1, /device:TPU:1, one launch (start us, length us, event | category | flops | bytes accessed | tf_op | source)
XLA Modules:
  0.0 215.2 jit_solution(1484289647478822760)
XLA Ops:
  0.7 94.6 %gather_and_forward.1 = (bf16[256,768]{1,0:T(8,128)(2,1)}, bf16[2,2,8,48,6144]{4,3,2,1,0:T(8,128)(2,1)}, bf16[2,2,8,192,768]{4,3,2,1,0:T(8,128)(2,1)}, f32[2,8,7...) custom-call(f32[2,24,2304]{2,1,0:T(8,128)} %refs_1_.1, ...), custom_call_target="tpu_custom_call" | custom-call | tf_op jit(solution)/shard_map/gather_and_forward/pallas_call | solution.py:601
  95.3 112.4 %backward_and_scatter.1 = (bf16[256,768]{1,0:T(8,128)(2,1)}, f32[2,24,6144]{2,1,0:T(8,128)}, bf16[2,96,768]{2,1,0:T(8,128)(2,1)}, f32[8,128]{1,0:T(8,128)}, bf16...) custom-call(bf16[256,768]{1,0:T(8,128)(2,1)} %bitcast.10, ...), custom_call_target="tpu_custom_call" | custom-call | tf_op jit(solution)/shard_map/backward_and_scatter/pallas_call | solution.py:1263
  207.7 7.1 %update.1 = (f32[2,24,2304]{2,1,0:T(8,128)}, f32[2,24,2304]{2,1,0:T(8,128)}, f32[2,24,2304]{2,1,0:T(8,128)}, bf16[2,24,2304]{2,1,0:T(8,128)(2,1)}, f32[2,24,768]...) custom-call(f32[2,24,6144]{2,1,0:T(8,128)} %get-tuple-element.79.ref, ...), custom_call_target="tpu_custom_call" | custom-call | tf_op jit(solution)/shard_map/update/pallas_call | solution.py:1356

commit v2 on v1

--- a/solution.py
+++ b/solution.py
@@ -106,9 +106,13 @@
         return self.sent[-1]
 
     def settle(self, most):
+        kept = []
         for copy in self.sent[:most]:
-            copy.wait_send()
-        del self.sent[:most]
+            if isinstance(copy, Batch) and copy.grows:
+                kept.append(copy)
+            else:
+                copy.wait_send()
+        self.sent = kept + self.sent[most:]
 
     def finish(self):
         self.settle(len(self.sent))
@@ -116,7 +120,7 @@
 
 class Batch:
     def __init__(self, net):
-        self.net, self.at, self.size = net, net.reserve(), 0
+        self.net, self.at, self.size, self.grows = net, net.reserve(), 0, False
 
     def put(self, src, dst, device):
         self.net.copy(src, dst, device, self.at).start()
@@ -355,15 +359,19 @@
                 chunk.aside = self.ring(chunk.spare, k - 1)
         if k == 2:
             chunk.shared = self.net.batch()
+            chunk.shared.grows = True
         if k >= 2:
             chunk.second[k - 2].wait_recv()
             for at in GROUPS[k - 2]:
                 if at is not None:
                     chunk.shared.put(chunk.whole(at), chunk.whole(at), self.sibling)
+            if k == 6:
+                chunk.shared.grows = False
 
     def nudge(self):
-        if self.done < len(self.turns):
-            i, k = self.turns[self.done]
+        for i, k in self.turns[self.done : self.done + 1]:
+            if self.done < EARLY:
+                self.net.settle(max(0, len(self.net.sent) - 16))
             self.tick(self.chunks[i], k)
             self.done += 1
 
@@ -371,12 +379,11 @@
         while (i, 6) not in self.turns[: self.done]:
             self.nudge()
         self.nudge()
-        if i == len(self.chunks) - 1:
-            self.net.settle(len(self.net.sent) - 4)
         self.chunks[i].shared.wait_recv()
 
 
-STARTS_AT = (0, 0.5, 2.5, 3, 4, 4.5)
+STARTS_AT = (0, 0.5, 2, 3, 4, 4.5)
+EARLY = 24
 GATHER_COPIES = 130
 SAVED = ("normed", "unit", "scales", "values", "probs", "mixed", "middle", "second", "hidden", "slope")
 
@@ -537,7 +544,8 @@
 
         for p in range(PAIRS):
             attend(p)
-            if p % 2:
+            if p % 3 == 2:
+                moves.nudge()
                 moves.nudge()
         save(layer, "unit", "scales", "probs", "mixed")
         middle[layer] = source[...].astype(F32) + dot(mixed[layer], wide(layer, 3 * D, D))
@@ -936,6 +944,7 @@
 REST = 4
 GAP = 3
 AT_ONCE = 5
+SETTLE, SETTLE_FIRST = 20, 8
 
 
 def buffer_shapes():
@@ -1164,7 +1173,7 @@
         head_sums = (zero, zero)
         for p in range(PAIRS):
             head_sums = attend(p, head_sums)
-            if p % 2:
+            if p % 3 == 2:
                 sums.turn()
         totals = []
         for part in head_sums:
@@ -1219,8 +1228,7 @@
 
     t = 0
     while sums.turn(0) or t < 7:
-        if sums.chunks[-2].at > 8:
-            net.settle(20)
+        net.settle(SETTLE if sums.chunks[-2].at > 8 else SETTLE_FIRST)
         arrive(norm_moving)
         norm_moving = []
         if t == 0:

time: 218 us -> 218 us (level)
  no operation moved by 1% of the time
where the time goes in v2:
time: 218 us; the launch traced here: 215 us
  Pallas kernels  214 us (98%)
    pallas_call x1, Pallas kernels, backward_pass(): pl.pallas_call(backward_kernel, out_shape=(jax.ShapeDtypeStruct((ROWS, D)...  114 us
    pallas_call x1, Pallas kernels, forward_pass(): pl.pallas_call(forward_kernel, out_shape=(jax.ShapeDtypeStruct((ROWS, D),...  93 us
    pallas_call x1, Pallas kernels, update(): pl.pallas_call(update_kernel, grid=(STEPS,), out_shape=[*shapes, *[jax.Sh...  7.11 us

profile of v2, /device:TPU:1, one launch (start us, length us, event | category | flops | bytes accessed | tf_op | source)
XLA Modules:
  0.0 214.9 jit_solution(2111759705664188151)
XLA Ops:
  0.7 93.0 %gather_and_forward.1 = (bf16[256,768]{1,0:T(8,128)(2,1)}, bf16[2,2,8,48,6144]{4,3,2,1,0:T(8,128)(2,1)}, bf16[2,2,8,192,768]{4,3,2,1,0:T(8,128)(2,1)}, f32[2,8,7...) custom-call(f32[2,24,2304]{2,1,0:T(8,128)} %refs_1_.1, ...), custom_call_target="tpu_custom_call" | custom-call | tf_op jit(solution)/shard_map/gather_and_forward/pallas_call | solution.py:609
  93.7 113.6 %backward_and_scatter.1 = (bf16[256,768]{1,0:T(8,128)(2,1)}, f32[2,24,6144]{2,1,0:T(8,128)}, bf16[2,96,768]{2,1,0:T(8,128)(2,1)}, f32[8,128]{1,0:T(8,128)}, bf16...) custom-call(bf16[256,768]{1,0:T(8,128)(2,1)} %bitcast.10, ...), custom_call_target="tpu_custom_call" | custom-call | tf_op jit(solution)/shard_map/backward_and_scatter/pallas_call | solution.py:1271
  207.4 7.1 %update.1 = (f32[2,24,2304]{2,1,0:T(8,128)}, f32[2,24,2304]{2,1,0:T(8,128)}, f32[2,24,2304]{2,1,0:T(8,128)}, bf16[2,24,2304]{2,1,0:T(8,128)(2,1)}, f32[2,24,768]...) custom-call(f32[2,24,6144]{2,1,0:T(8,128)} %get-tuple-element.79.ref, ...), custom_call_target="tpu_custom_call" | custom-call | tf_op jit(solution)/shard_map/update/pallas_call | solution.py:1364
